TPU v7x, 128 devices: a whole 4x4x4 slice. The times are simulated.
128 devices in a mesh: dp: 32 (over y, z, core), ctx: 4 (over x).
Axes of the slice: x: 4, y: 4, z: 4, core: 2. Of those that a mesh axis runs over, the one named last changes fastest.
Arguments:
- tokens: bfloat16 [16384, 1024], P(('dp', 'ctx')), may hold values from -6 to 6
- cotangent: bfloat16 [16384, 1024], P(('dp', 'ctx')), may hold values from -6 to 6
- packed_pos: int32 [16384], P(('dp', 'ctx')), may hold values from 0 to 16383, as said below
- segment_ids: int32 [32, 512], P('dp'), may hold values from 0 to 7, never falling along the last dimension, each value on 1 to 256 neighbouring positions
- w_proj: bfloat16 [1024, 16, 256], P(None, 'ctx'), may hold values from -0.1875 to 0.1875
- w_out: bfloat16 [1024, 1024], replicated, may hold values from -0.1875 to 0.1875
Outputs:
- layer_out: bfloat16 [16384, 1024], P(('dp', 'ctx'))
- input_grad: bfloat16 [16384, 1024], P(('dp', 'ctx'))
- proj_grad: float32 [1024, 16, 256], P(None, 'ctx')
- out_grad: float32 [1024, 1024], P('ctx')
Inputs may be any that keep to these rules, and one draw needn't show every extreme that they name: packed_pos is a permutation that keeps each row's index of ctx; the rows of one device go to every index of dp, at most 6 rows to any one of them, and every device receives 128 rows.
All inputs are finite; a program needn't handle non-finite values.
Results may differ from a plain program's by a relative error of at most 0.02.
Values may be sent and summed in bfloat16 or wider, within the bound.
A program may use at most 128 MiB of HBM per device.

v0:
```python
import jax
import jax.numpy as jnp
from jax import lax
from jax.sharding import PartitionSpec as P

EPS = 1e-05


def silu_slope(t):
    sig = jax.nn.sigmoid(t)
    return sig * (1.0 + t * (1.0 - sig))


def block_mask(seg, start, block):
    rows_here = start + jnp.arange(block, dtype=jnp.int32)
    keys_all = jnp.arange(seg.shape[0], dtype=jnp.int32)
    return (seg[:, None] == seg[None, :]) & (keys_all[None, :] <= rows_here[:, None])


def attend(query, keys, values, seg, alpha, block):
    count = query.shape[0] // block

    def one_block(index):
        start = index * block
        score = alpha * jnp.einsum("ihd,jhd->hij", query, keys, preferred_element_type=jnp.float32)
        mask = block_mask(seg, start, block)
        weight = jnp.where(mask[None], jax.nn.silu(score), 0.0).astype(jnp.bfloat16)
        return jnp.einsum("hij,jhd->ihd", weight, values, preferred_element_type=jnp.float32)

    outs = lax.map(one_block, jnp.arange(count, dtype=jnp.int32))
    return outs.reshape(query.shape)


def attend_grad(query, keys, values, d_out, seg, alpha, block):
    count = query.shape[0] // block

    def one_block(carry, index):
        d_keys, d_values = carry
        start = index * block
        score = alpha * jnp.einsum("ihd,jhd->hij", query, keys, preferred_element_type=jnp.float32)
        mask = block_mask(seg, start, block)[None]
        weight = jnp.where(mask, jax.nn.silu(score), 0.0).astype(jnp.bfloat16)
        d_weight = jnp.einsum("ihd,jhd->hij", d_out, values, preferred_element_type=jnp.float32)
        d_values = d_values + jnp.einsum(
            "hij,ihd->jhd", weight, d_out, preferred_element_type=jnp.float32
        )
        d_score = jnp.where(mask, d_weight * silu_slope(score) * alpha, 0.0).astype(jnp.bfloat16)
        d_query = jnp.einsum("hij,jhd->ihd", d_score, keys, preferred_element_type=jnp.float32)
        d_keys = d_keys + jnp.einsum(
            "hij,ihd->jhd", d_score, query, preferred_element_type=jnp.float32
        )
        return ((d_keys, d_values), d_query)

    zeros = jnp.zeros(query.shape, jnp.float32)
    (d_keys, d_values), d_query = lax.scan(
        one_block, (zeros, zeros), jnp.arange(count, dtype=jnp.int32)
    )
    return (d_query.reshape(query.shape), d_keys, d_values)


def shards(tokens, cotangent, packed_pos, segment_ids, w_proj, w_out):
    rows, width = tokens.shape
    n_data = lax.axis_size("dp")
    n_group = lax.axis_size("ctx")
    group = rows * n_group
    capacity = 3 * rows // (2 * n_data)
    total_slots = n_data * capacity
    heads_dev = w_proj.shape[1]
    head_size = w_proj.shape[2] // 4
    block = 512
    alpha = head_size ** (-0.5)
    target = packed_pos // group
    target_row = packed_pos % rows
    onehot = (target[:, None] == jnp.arange(n_data, dtype=jnp.int32)[None, :]).astype(jnp.int32)
    before = jnp.cumsum(onehot, axis=0) - onehot
    slot = target * capacity + jnp.sum(before * onehot, axis=1)
    send_x = jnp.zeros((total_slots, width), jnp.bfloat16).at[slot].set(tokens)
    send_g = jnp.zeros((total_slots, width), jnp.bfloat16).at[slot].set(cotangent)
    send_rows = jnp.full((total_slots,), -1, jnp.int32).at[slot].set(target_row)
    recv_x, recv_g, arrive = (
        lax.all_to_all(send_x, "dp", split_axis=0, concat_axis=0, tiled=True),
        lax.all_to_all(send_g, "dp", split_axis=0, concat_axis=0, tiled=True),
        lax.all_to_all(send_rows, "dp", split_axis=0, concat_axis=0, tiled=True),
    )
    placed = jnp.where(arrive < 0, rows, arrive)
    packed_x = jnp.zeros((rows, width), jnp.bfloat16).at[placed].set(recv_x, mode="drop")
    packed_g = jnp.zeros((rows, width), jnp.bfloat16).at[placed].set(recv_g, mode="drop")
    source_row = jnp.clip(arrive, 0, rows - 1)
    live = (arrive >= 0)[:, None]

    def outgoing(values):
        return jnp.where(live, values[source_row], jnp.zeros((), values.dtype))

    input_float = packed_x.astype(jnp.float32)
    first_mean1 = jnp.mean(input_float, axis=1, keepdims=True)
    inverse_deviation = lax.rsqrt(
        jnp.mean((input_float - first_mean1) ** 2, axis=1, keepdims=True) + EPS
    )
    centered_scaled_input = (input_float - first_mean1) * inverse_deviation
    layer_normalized = centered_scaled_input.astype(jnp.bfloat16)
    whole_normed = lax.all_gather(layer_normalized, "ctx", axis=0, tiled=True)
    w_local = w_proj.reshape(width, heads_dev * 4 * head_size)
    pre = jnp.dot(whole_normed, w_local, preferred_element_type=jnp.float32)
    act = jax.nn.silu(pre).astype(jnp.bfloat16).reshape(group, heads_dev, 4, head_size)
    gate_u, val, query, keys = (act[:, :, 0], act[:, :, 1], act[:, :, 2], act[:, :, 3])
    seg = segment_ids[0]
    attn_heads = (
        attend(query, keys, val, seg, alpha, block)
        .astype(jnp.bfloat16)
        .reshape(group, heads_dev * head_size)
    )
    gate_heads = gate_u.reshape(group, heads_dev * head_size)
    attn_tok, gate_tok = (
        lax.all_to_all(attn_heads, "ctx", split_axis=0, concat_axis=1, tiled=True),
        lax.all_to_all(gate_heads, "ctx", split_axis=0, concat_axis=1, tiled=True),
    )
    a_f = attn_tok.astype(jnp.float32)
    mean2 = jnp.mean(a_f, axis=1, keepdims=True)
    r_two = lax.rsqrt(jnp.mean((a_f - mean2) ** 2, axis=1, keepdims=True) + EPS)
    onorm = (a_f - mean2) * r_two
    u_f = gate_tok.astype(jnp.float32)
    gated = (onorm * u_f).astype(jnp.bfloat16)
    y_packed = (input_float + jnp.dot(gated, w_out, preferred_element_type=jnp.float32)).astype(
        jnp.bfloat16
    )
    dgated = jnp.dot(packed_g, w_out.T, preferred_element_type=jnp.float32)
    d_gate = (dgated * onorm).astype(jnp.bfloat16)
    e_term = dgated * u_f
    d_attn = (
        r_two
        * (
            e_term
            - jnp.mean(e_term, axis=1, keepdims=True)
            - onorm * jnp.mean(e_term * onorm, axis=1, keepdims=True)
        )
    ).astype(jnp.bfloat16)
    d_attn_heads, d_gate_heads = (
        lax.all_to_all(d_attn, "ctx", split_axis=1, concat_axis=0, tiled=True),
        lax.all_to_all(d_gate, "ctx", split_axis=1, concat_axis=0, tiled=True),
    )
    d_query, d_keys, d_values = attend_grad(
        query, keys, val, d_attn_heads.reshape(group, heads_dev, head_size), seg, alpha, block
    )
    d_act = jnp.stack(
        [
            d_gate_heads.reshape(group, heads_dev, head_size).astype(jnp.float32),
            d_values,
            d_query,
            d_keys,
        ],
        axis=2,
    )
    d_pre = (d_act.reshape(group, heads_dev * 4 * head_size) * silu_slope(pre)).astype(jnp.bfloat16)
    proj_term = jnp.dot(whole_normed.T, d_pre, preferred_element_type=jnp.float32)
    normalized_gradient = lax.psum_scatter(
        jnp.dot(d_pre, w_local.T, preferred_element_type=jnp.float32).astype(jnp.bfloat16),
        "ctx",
        scatter_dimension=0,
        tiled=True,
    ).astype(jnp.float32)
    dx_packed = (
        packed_g.astype(jnp.float32)
        + inverse_deviation
        * (
            normalized_gradient
            - jnp.mean(normalized_gradient, axis=1, keepdims=True)
            - centered_scaled_input
            * jnp.mean(normalized_gradient * centered_scaled_input, axis=1, keepdims=True)
        )
    ).astype(jnp.bfloat16)
    scale = (rows * n_group * n_data) ** (-0.5)
    head_rows = heads_dev * head_size
    full_out = lax.psum(
        jnp.dot(gated.T, packed_g, preferred_element_type=jnp.float32), ("dp", "ctx")
    )
    out_sum = lax.dynamic_slice_in_dim(full_out, lax.axis_index("ctx") * head_rows, head_rows, 0)
    proj_sum = lax.psum(proj_term.astype(jnp.bfloat16), "dp").astype(jnp.float32)
    back_y, back_dx = (
        lax.all_to_all(outgoing(y_packed), "dp", split_axis=0, concat_axis=0, tiled=True),
        lax.all_to_all(outgoing(dx_packed), "dp", split_axis=0, concat_axis=0, tiled=True),
    )
    layer_out = back_y[slot]
    input_grad = back_dx[slot]
    return (layer_out, input_grad, (proj_sum * scale).reshape(w_proj.shape), out_sum * scale)


def solution(mesh):
    return jax.shard_map(
        shards,
        mesh=mesh,
        in_specs=(
            P(("dp", "ctx"), None),
            P(("dp", "ctx"), None),
            P(("dp", "ctx")),
            P("dp", None),
            P(None, "ctx", None),
            P(),
        ),
        out_specs=(
            P(("dp", "ctx"), None),
            P(("dp", "ctx"), None),
            P(None, "ctx", None),
            P("ctx", None),
        ),
        check_vma=False,
    )
```

profile of v0, /device:TPU:1, one launch (start us, length us, event | category | flops | bytes accessed | tf_op | source)
XLA Modules:
  0.0 466.1 jit_solution(2791168478216192747)
XLA Ops:
  10.2 9.6 %all-to-all-start = ((s32[32,6,1]{1,2,0:T(1,128)}), s32[32,6,1]{1,2,0:T(1,128)S(1)}, u32[]{:S(2)}, u32[]{:S(2)}) async-start(s32[32,6,1]{1,2,0:T(1,128)} %bitcast), calls=%async_computation | async-start | bytes 32768 | tf_op jit(solution)/shard_map/all_to_all | solution.py:83
  22.4 4.3 all-to-all-done
  26.6 4.2 all-to-all-start.1
  32.2 10.4 %all-to-all-done.1 = bf16[32,6,1024]{2,1,0:T(8,128)(2,1)S(1)} async-done(((bf16[32,6,1024]{2,1,0:T(8,128)(2,1)}), bf16[32,6,1024]{2,1,0:T(8,128)(2,1)S(1)}, u32[]{:S(2)}, u32[]{:S(2)}) %all-to-all-start.1) | async-done | bytes 393248 | tf_op jit(solution)/shard_map/all_to_all | solution.py:81
  48.1 4.4 all-to-all-start.5
  52.5 3.5 copy.67
  57.0 8.9 %all-gather.2.cloned.1.call-done = bf16[512,1024]{1,0:T(8,128)(2,1)} async-done(((bf16[128,1024]{1,0:T(8,128)(2,1)}), bf16[512,1024]{1,0:T(8,128)(2,1)}) %all-gather.2.cloned.1.call-update) | async-done | bytes 1048592 | tf_op jit(solution)/shard_map/all_gather | solution.py:101
  65.8 5.0 %multiply_convert_fusion.1 = (bf16[512,1024]{1,0:T(8,128)(2,1)}, f32[512,1024]{1,0:T(8,128)}) fusion(bf16[512,1024]{1,0:T(8,128)(2,1)} %all-gather.2.cloned.1.call-done, bf16[1024,1024]{1,0:T(8,128)(2,1)} %bitcast.100), kind=kOutput, calls=%fused_computation.15 | convolution fusion | flops 1076363264 | bytes 6291456 | tf_op jit(solution)/shard_map/dot_general | solution.py:103
  72.4 4.8 %select_convert_fusion.1 = (bf16[4,512,512]{2,1,0:T(8,128)(2,1)S(1)}, f32[4,512,512]{2,1,0:T(8,128)}) fusion(pred[512,512]{1,0:T(8,128)(4,1)} %fusion.2, bf16[512,4,4,64]{0,3,2,1:T(8,128)(2,1)S(1)} %bitcast.93), kind=kOutput, calls=%fused_computation.11 | convolution fusion | flops 141557760 | bytes 7077888 | tf_op jit(solution)/shard_map/while/body/eval_jaxpr/ihd,jhd->hij/dot_general | solution.py:25
  81.7 3.4 all-to-all-start.2
  90.6 4.2 all-to-all-start.3
  97.2 3.0 all-to-all-done.3
  104.0 2.6 fusion.25
  107.6 3.4 all-to-all-start.7
  112.7 3.8 all-to-all-done.7
  116.5 4.0 all-to-all-start.6
  120.9 3.0 convolution_bitcast_fusion.2
  123.9 4.1 select_convert_fusion
  137.1 2.9 copy.59
  140.1 3.1 multiply_convert_fusion
  144.2 2.3 convolution_convert_fusion.1
  146.5 4.2 convolution_convert_fusion
  150.9 2.7 fusion.26
  156.1 18.7 %reduce-scatter.2.cloned.1.call-done = bf16[128,1024]{1,0:T(8,128)(2,1)} async-done(((bf16[512,1024]{1,0:T(8,128)(2,1)}), bf16[128,1024]{1,0:T(8,128)(2,1)}) %reduce-scatter.2.cloned.1.call-update) | async-done | bytes 262160 | tf_op jit(solution)/shard_map/reduce_scatter | solution.py:155
  181.4 9.0 %all-to-all-start.8 = ((bf16[32,6,1024]{2,1,0:T(8,128)(2,1)}), bf16[32,6,1024]{2,1,0:T(8,128)(2,1)S(1)}, u32[]{:S(2)}, u32[]{:S(2)}) async-start(bf16[32,6,1024]{2,1,0:T(8,128)(2,1)} %get-tuple-element.47), calls=%async_computation.9 | async-start | bytes 1048576 | tf_op jit(solution)/shard_map/all_to_all | solution.py:180
  190.5 12.6 %all-to-all-done.8 = bf16[32,6,1024]{2,1,0:T(8,128)(2,1)S(1)} async-done(((bf16[32,6,1024]{2,1,0:T(8,128)(2,1)}), bf16[32,6,1024]{2,1,0:T(8,128)(2,1)S(1)}, u32[]{:S(2)}, u32[]{:S(2)}) %all-to-all-start.8) | async-done | bytes 393248 | tf_op jit(solution)/shard_map/all_to_all | solution.py:180
  203.1 4.4 all-to-all-start.4
  207.5 86.0 %all-reduce.3.cloned.1.call-done = bf16[1024,1024]{1,0:T(8,128)(2,1)} async-done(((bf16[1024,1024]{1,0:T(8,128)(2,1)}), bf16[1024,1024]{1,0:T(8,128)(2,1)}) %all-reduce.3.cloned.1.call-update) | async-done | bytes 2097168 | tf_op jit(solution)/shard_map/psum | solution.py:177
  293.5 4.2 convert_multiply_fusion
  297.7 5.6 %reshape.236 = f32[1024,4,256]{2,1,0:T(4,128)} reshape(f32[1024,1024]{1,0:T(8,128)} %convert_multiply_fusion) | data formatting | bytes 8388608 | tf_op jit(solution)/shard_map/reshape | solution.py:184
  303.3 149.5 %all-reduce.5.cloned.1.call-done = f32[1024,1024]{1,0:T(8,128)} async-done(((f32[1024,1024]{1,0:T(8,128)}), f32[1024,1024]{1,0:T(8,128)}) %all-reduce.5.cloned.1.call-update) | async-done | bytes 4194320 | tf_op jit(solution)/shard_map/psum | solution.py:173
  452.8 2.3 dynamic-slice_multiply_fusion
  (106 shorter events, 57.9 us)
Async XLA Ops:
  7.2 96.9 %copy-start = (bf16[1024,1024]{1,0:T(8,128)(2,1)S(1)}, bf16[1024,1024]{1,0:T(8,128)(2,1)}, u32[]{:S(2)}) copy-start(bf16[1024,1024]{1,0:T(8,128)(2,1)} %param.11) | copy-start | bytes 6291460
  8.4 37.0 %copy-start.9 = (s32[128]{0:T(128)}, s32[128]{0:T(128)S(1)}, u32[]{:S(2)}) copy-start(s32[128]{0:T(128)S(1)} %compare_select_fusion.3) | copy-start | bytes 1540
  10.2 16.5 %all-to-all-start = ((s32[32,6,1]{1,2,0:T(1,128)}), s32[32,6,1]{1,2,0:T(1,128)S(1)}, u32[]{:S(2)}, u32[]{:S(2)}) async-start(s32[32,6,1]{1,2,0:T(1,128)} %bitcast), calls=%async_computation | async-start | bytes 32768 | tf_op jit(solution)/shard_map/all_to_all | solution.py:83
  26.6 15.9 %all-to-all-start.1 = ((bf16[32,6,1024]{2,1,0:T(8,128)(2,1)}), bf16[32,6,1024]{2,1,0:T(8,128)(2,1)S(1)}, u32[]{:S(2)}, u32[]{:S(2)}) async-start(bf16[32,6,1024]{2,1,0:T(8,128)(2,1)} %all_to_all.79), calls=%async_computation.1 | async-start | bytes 1048576 | tf_op jit(solution)/shard_map/all_to_all | solution.py:81
  30.8 35.0 %all-gather.2.cloned.1.call-start = ((), (), s32[]{:S(2)}) async-start(), calls=%async_computation.10 | async-start | bytes 1310720 | tf_op jit(solution)/shard_map/all_gather | solution.py:101
  48.1 33.6 %all-to-all-start.5 = ((bf16[32,6,1024]{2,1,0:T(8,128)(2,1)}), bf16[32,6,1024]{2,1,0:T(8,128)(2,1)}, u32[]{:S(2)}, u32[]{:S(2)}) async-start(bf16[32,6,1024]{2,1,0:T(8,128)(2,1)} %all_to_all.87), calls=%async_computation.5 | async-start | bytes 1048576 | tf_op jit(solution)/shard_map/all_to_all | solution.py:82
  52.5 3.6 copy-start.8
  72.3 4.8 %copy-start.2 = (bf16[512,1024]{0,1:T(8,128)(2,1)}, bf16[512,1024]{0,1:T(8,128)(2,1)S(1)}, u32[]{:S(2)}) copy-start(bf16[512,1024]{0,1:T(8,128)(2,1)S(1)} %copy.46) | copy-start | bytes 3145732
  77.1 1.3 copy-start.1
  81.7 8.9 %all-to-all-start.2 = ((bf16[4,128,256]{1,2,0:T(8,128)(2,1)}), bf16[4,128,256]{1,2,0:T(8,128)(2,1)S(1)}, u32[]{:S(2)}, u32[]{:S(2)}) async-start(bf16[4,128,256]{1,2,0:T(8,128)(2,1)} %copy.50), calls=%async_computation.2 | async-start | bytes 524288 | tf_op jit(solution)/shard_map/all_to_all | solution.py:114
  90.6 9.6 %all-to-all-start.3 = ((bf16[4,128,256]{1,2,0:T(8,128)(2,1)}), bf16[4,128,256]{1,2,0:T(8,128)(2,1)}, u32[]{:S(2)}, u32[]{:S(2)}) async-start(bf16[4,128,256]{1,2,0:T(8,128)(2,1)} %copy.52), calls=%async_computation.3 | async-start | bytes 524288 | tf_op jit(solution)/shard_map/all_to_all | solution.py:115
  107.6 8.9 %all-to-all-start.7 = ((bf16[128,4,256]{2,0,1:T(8,128)(2,1)}), bf16[128,4,256]{2,0,1:T(8,128)(2,1)S(1)}, u32[]{:S(2)}, u32[]{:S(2)}) async-start(bf16[128,4,256]{2,0,1:T(8,128)(2,1)} %bitcast.90), calls=%async_computation.7 | async-start | bytes 524288 | tf_op jit(solution)/shard_map/all_to_all | solution.py:138
  116.5 14.3 %all-to-all-start.6 = ((bf16[128,4,256]{2,0,1:T(8,128)(2,1)}), bf16[128,4,256]{2,0,1:T(8,128)(2,1)}, u32[]{:S(2)}, u32[]{:S(2)}) async-start(bf16[128,4,256]{2,0,1:T(8,128)(2,1)} %bitcast.91), calls=%async_computation.6 | async-start | bytes 524288 | tf_op jit(solution)/shard_map/all_to_all | solution.py:139
  120.6 54.3 %reduce-scatter.2.cloned.1.call-start = ((), (), s32[]{:S(2)}) async-start(), calls=%async_computation.11 | async-start | bytes 1310720 | tf_op jit(solution)/shard_map/reduce_scatter | solution.py:155
  120.9 3.0 copy-start.3
  120.9 3.0 copy-start.7
  140.1 4.1 copy-start.4
  143.2 1.0 copy-start.6
  146.5 147.0 %all-reduce.3.cloned.1.call-start = ((), (), s32[]{:S(2)}) async-start(), calls=%async_computation.12 | async-start | bytes 4194304 | tf_op jit(solution)/shard_map/psum | solution.py:177
  150.7 302.1 %all-reduce.5.cloned.1.call-start = ((), (), s32[]{:S(2)}) async-start(), calls=%async_computation.13 | async-start | bytes 8388608 | tf_op jit(solution)/shard_map/psum | solution.py:173
  177.3 2.0 copy-start.5
  178.3 12.2 %copy-start.10 = (s32[128]{0:T(128)S(1)}, s32[128]{0:T(128)}, u32[]{:S(2)}) copy-start(s32[128]{0:T(128)} %copy-done.9) | copy-start | bytes 1540
  181.4 21.7 %all-to-all-start.8 = ((bf16[32,6,1024]{2,1,0:T(8,128)(2,1)}), bf16[32,6,1024]{2,1,0:T(8,128)(2,1)S(1)}, u32[]{:S(2)}, u32[]{:S(2)}) async-start(bf16[32,6,1024]{2,1,0:T(8,128)(2,1)} %get-tuple-element.47), calls=%async_computation.9 | async-start | bytes 1048576 | tf_op jit(solution)/shard_map/all_to_all | solution.py:180
  203.1 253.7 %all-to-all-start.4 = ((bf16[32,6,1024]{2,1,0:T(8,128)(2,1)}), bf16[32,6,1024]{2,1,0:T(8,128)(2,1)}, u32[]{:S(2)}, u32[]{:S(2)}) async-start(bf16[32,6,1024]{2,1,0:T(8,128)(2,1)} %get-tuple-element.48), calls=%async_computation.4 | async-start | bytes 1048576 | tf_op jit(solution)/shard_map/all_to_all | solution.py:179
Sparse Core Ops, SparseCore 0:
  45.6 20.2 all-gather.1
  146.6 28.2 reduce-scatter.1
  179.1 114.3 all-reduce.2
  299.1 153.6 all-reduce.4
where the time goes:
time: 468 us; the launch traced here: 466 us
  waiting for transfers between devices  298 us (64%)
  local copies, waits for them, and re-layouts  49.5 us (11%)
  starting transfers between devices  46.9 us (10%)
  matrix products  33.2 us (7%)
  other arithmetic  24 us (5%)
  between operations  14.2 us (3%)
    psum x1, waiting for transfers between devices, shards(): lax.psum(jnp.dot(gated.T, packed_g, preferred_element_type=jnp.float32),...  150 us
    psum x1, waiting for transfers between devices, shards(): lax.psum(proj_term.astype(jnp.bfloat16), 'dp').astype(jnp.float32)  86 us
    reduce_scatter x1, waiting for transfers between devices, shards(): lax.psum_scatter(jnp.dot(d_pre, w_local.T, preferred_element_type=jnp.flo...  18.7 us
    all_to_all x1, waiting for transfers between devices, shards(): lax.all_to_all(outgoing(dx_packed), 'dp', split_axis=0, concat_axis=0, ti...  12.6 us
    all_to_all x1, waiting for transfers between devices, shards(): lax.all_to_all(send_x, 'dp', split_axis=0, concat_axis=0, tiled=True)  10.4 us
    all_to_all x1, starting transfers between devices, shards(): lax.all_to_all(send_rows, 'dp', split_axis=0, concat_axis=0, tiled=True)  9.6 us
  transfers between devices with their start and end apart: 13, of which 10 were waited for; matrix products, arithmetic and copies ran while one was open for 15% of the time, Pallas kernels for 0%

commit v1 on v0

v1 whole, which is shorter than its diff:
```python
import functools
import jax
import jax.numpy as jnp
from jax import lax
from jax.experimental import pallas as pl
from jax.experimental.pallas import tpu as pltpu
from jax.sharding import PartitionSpec as P

EPS = 1e-05
MESH = pl.DeviceIdType.MESH
bf16, f32, i32 = jnp.bfloat16, jnp.float32, jnp.int32
ROWS, WIDTH, GROUP, SLOTS = 128, 1024, 512, 16
CAP = 6
COMBOS = [(L, c) for L in range(3) for c in range(8) if c * CAP < 16 * L + 16 and c * CAP + CAP > 16 * L]
PIECES = 5


def dot(a, b):
    return lax.dot_general(a, b, (((1,), (0,)), ((), ())), preferred_element_type=f32)


def dot_nt(a, b):
    return lax.dot_general(a, b, (((1,), (1,)), ((), ())), preferred_element_type=f32)


def dot_tn(a, b):
    return lax.dot_general(a, b, (((0,), (0,)), ((), ())), preferred_element_type=f32)


def sigmoid(t):
    return 0.5 * jnp.tanh(0.5 * t) + 0.5


def iota(shape, axis):
    return lax.broadcasted_iota(i32, shape, axis)


def one(cond):
    return jnp.where(cond, 1.0, 0.0).astype(bf16)


def chunk(c):
    return pl.ds(c * 128, 128)


def kernel(
    n_dp, stop,
    tok, cot, pos_ref, seg_ref, w, wo,
    y_out, dx_out, ar_f,
    send_x, recv_x, send_g, recv_g, send_y, recv_y, send_d, recv_d,
    meta_t, rank_s, xp, xhat, rstd_ref, nrm, nrm_t, gbuf,
    msk, slope, uv, qk, kq, qz, p_ref, sl_ref, ds_ref, dq_ref,
    attn_ref, u_ref, dg_ref, st_all, cmb, gated, gfull, dout, du_ref, dpre,
    yd, ar_src, ar_c, ar_h, ar_r, rs_send, rs_own, rs1, rs2,
    a2a_s, a2a_r, ag_s, ag_r, st_s, st_r, gt_s, gt_r, s1_s, s1_r, s2_s, s2_r, s3_s, s3_r, s4_s, s4_r, rs_s, rs_r,
):
    me, cx = lax.axis_index("dp"), lax.axis_index("ctx")
    core, chip = lax.rem(me, 2), lax.div(me, 2)
    other = 1 - core
    n_chip = n_dp // 2
    right, left, opp = lax.rem(cx + 1, 4), lax.rem(cx + 3, 4), lax.rem(cx + 2, 4)
    sends = []

    def rc(src, dst, ss, rs, dev):
        return pltpu.make_async_remote_copy(
            src_ref=src, dst_ref=dst, send_sem=ss, recv_sem=rs, device_id=dev, device_id_type=MESH
        )

    def wait_bytes(ref, ss, rs):
        return rc(ref, ref, ss, rs, {"ctx": right})

    def al(i, m):
        return pl.multiple_of(i * m, m)

    bar = pltpu.get_barrier_semaphore()

    @pl.loop(1, n_dp)
    def _(o):
        pl.semaphore_signal(bar, inc=1, device_id={"dp": lax.rem(me + o, n_dp)}, device_id_type=MESH)

    for o in range(1, 4):
        pl.semaphore_signal(bar, inc=1, device_id={"ctx": lax.rem(cx + o, 4)}, device_id_type=MESH)

    pos_l = jnp.broadcast_to(pos_ref[...], (ROWS, ROWS))
    pos_s = jnp.transpose(pos_l.astype(f32)).astype(i32)
    tgt_l, tgt_s = lax.shift_right_logical(pos_l, 9), lax.shift_right_logical(pos_s, 9)
    ii, jj = iota((ROWS, ROWS), 0), iota((ROWS, ROWS), 1)
    same = tgt_l == tgt_s
    rank_l = jnp.sum(jnp.where(same & (ii < jj), 1.0, 0.0), axis=0, keepdims=True).astype(i32)
    rank_c = jnp.sum(jnp.where(same & (jj < ii), 1.0, 0.0), axis=1, keepdims=True).astype(i32)
    tgt_row = tgt_l[:1] * SLOTS
    rank_s[...] = jnp.where(jj == 0, rank_c, tgt_s * SLOTS)
    row_no = (pos_s & (ROWS - 1)) + 1

    def pack_out(src, dst, with_meta):
        @pl.loop(0, 4)
        def _(rb):
            rows = pl.ds(al(rb, 128), 128)
            here = iota((128, ROWS), 0) + rb * 128
            meta = jnp.zeros((128, 128), f32)
            for L in range(3):
                acc = jnp.zeros((128, 128), f32)
                every = jnp.zeros((128, 128), f32)
                for c in [c for (l, c) in COMBOS if l == L]:
                    v = rank_l + (c * CAP - 16 * L)
                    idx = jnp.where((v >= 0) & (v < 16), tgt_row + v, -1)
                    hit = jnp.where(here == idx, 1.0, 0.0)
                    acc = acc + dot(hit.astype(bf16), src[:, c * 128:c * 128 + 128])
                    every = every + hit
                dst[rows, L * 128:L * 128 + 128] = acc.astype(bf16)
                if with_meta:
                    meta = meta + dot(every.astype(bf16), jnp.where(jj == L, row_no, 0).astype(f32).astype(bf16))
            if with_meta:
                dst[rows, 384:512] = meta.astype(bf16)

    def a2a_start(k, src, dst):
        mine = pl.ds(al(me, SLOTS), SLOTS)
        dst[mine, :] = src[mine, :]

        @pl.loop(1, n_dp)
        def _(o):
            t = lax.rem(me + o, n_dp)
            rc(src.at[pl.ds(al(t, SLOTS), SLOTS)], dst.at[mine], a2a_s.at[k], a2a_r.at[k], {"dp": t}).start()

        part = src.at[pl.ds(0, (n_dp - 1) * SLOTS)]
        sends.append(lambda: wait_bytes(part, a2a_s.at[k], a2a_r.at[k]).wait_send())

    def a2a_wait(k, dst):
        wait_bytes(dst.at[pl.ds(0, (n_dp - 1) * SLOTS)], a2a_s.at[k], a2a_r.at[k]).wait_recv()

    def unpack_arrived(src, dst, rows):
        unit = iota((ROWS, 512), 1) & 15
        for c in range(8):
            acc = jnp.zeros((ROWS, 128), f32)
            for L in [l for (l, d) in COMBOS if d == c]:
                lo = c * CAP - 16 * L
                hit = (meta_t[L:L + 1, :] == (iota((ROWS, 512), 0) + 1).astype(f32)) & (unit >= lo) & (unit < lo + CAP)
                acc = acc + dot(one(hit), src[:, L * 128:L * 128 + 128])
            dst[rows, c * 128:c * 128 + 128] = acc.astype(bf16)

    def pack_back(src, dst):
        @pl.loop(0, 4)
        def _(rb):
            rows = pl.ds(al(rb, 128), 128)
            meta = recv_x[rows, 384:512].astype(f32)
            unit = iota((128, ROWS), 0) & 15
            lane = (iota((128, ROWS), 1) + 1).astype(f32)
            for L in range(3):
                acc = jnp.zeros((128, 128), f32)
                mine = meta[:, L:L + 1] == lane
                for c in [c for (l, c) in COMBOS if l == L]:
                    lo = c * CAP - 16 * L
                    acc = acc + dot(one(mine & (unit >= lo) & (unit < lo + CAP)), src[:, c * 128:c * 128 + 128])
                dst[rows, L * 128:L * 128 + 128] = acc.astype(bf16)

    def unpack_home(src, dst):
        rank, base = rank_s[:, 0:1], rank_s[:, 1:2]
        lanes = iota((ROWS, 512), 1)
        for c in range(8):
            acc = jnp.zeros((ROWS, 128), f32)
            for L in [l for (l, d) in COMBOS if d == c]:
                v = rank + (c * CAP - 16 * L)
                idx = jnp.where((v >= 0) & (v < 16), base + v, -1)
                acc = acc + dot(one(lanes == idx), src[:, L * 128:L * 128 + 128])
            dst[:, c * 128:c * 128 + 128] = acc.astype(bf16)

    def finish():
        for f in sends:
            f()

    pack_out(tok, send_x, True)
    pl.semaphore_wait(bar, n_dp - 1 + 3)
    a2a_start(0, send_x, recv_x)
    pack_out(cot, send_g, False)
    a2a_start(1, send_g, recv_g)

    seg_row = seg_ref[...]
    seg_col = jnp.transpose(jnp.broadcast_to(seg_row.astype(f32), (128, GROUP))).astype(i32)
    for b in range(4):
        sc = seg_col[b * 128:b * 128 + 128, 0:1]
        ok = (sc == seg_row) & (iota((128, GROUP), 1) <= iota((128, GROUP), 0) + b * 128)
        msk[b * 128:b * 128 + 128, :] = jnp.where(ok, 1.0, 0.0)
    cmb[...] = jnp.zeros_like(cmb)

    own = pl.ds(al(cx, 128), 128)
    a2a_wait(0, recv_x)
    meta_t[...] = jnp.transpose(recv_x[:, 384:512].astype(f32))[:8]
    unpack_arrived(recv_x, xp, pl.ds(0, 128))
    xf = xp[...].astype(f32)
    mean = jnp.mean(xf, axis=1, keepdims=True)
    rstd = lax.rsqrt(jnp.mean((xf - mean) ** 2, axis=1, keepdims=True) + EPS)
    xh = (xf - mean) * rstd
    xhat[...] = xh
    rstd_ref[...] = jnp.broadcast_to(rstd, (ROWS, 128))
    nrm[own, :] = xh.astype(bf16)

    def half(b, k):
        return pl.ds(pl.multiple_of(b * 128 + k * 64, 64), 64)

    def ag(k, buf):
        def to(block, h, way, slot):
            ref = buf.at[half(block, h)]
            return rc(ref, ref, ag_s.at[k], ag_r.at[k, slot], {"ctx": way})

        def start():
            to(cx, 0, right, 0).start()
            to(cx, 1, left, 1).start()
            to(cx, 1, right, 2).start()
            to(cx, 0, left, 3).start()

        def forward():
            to(left, 0, right, 0).wait_recv()
            to(left, 0, right, 4).start()
            to(right, 1, left, 1).wait_recv()
            to(right, 1, left, 5).start()
            sends.append(lambda: wait_bytes(buf.at[pl.ds(0, 384)], ag_s.at[k], ag_r.at[k, 0]).wait_send())

        def near():
            to(left, 1, right, 2).wait_recv()
            to(right, 0, left, 3).wait_recv()

        def far():
            to(opp, 0, right, 4).wait_recv()
            to(opp, 1, left, 5).wait_recv()

        return start, forward, near, far

    lane_lo = iota((128, 128), 1) < 64

    def project(block):
        rows = pl.ds(al(block, 128), 128)
        nT = jnp.transpose(nrm[rows, :].astype(f32)).astype(bf16)
        nrm_t[block] = nT

        @pl.loop(0, 4)
        def _(h):
            pre = dot(nrm[rows, :], w[h])
            sig = sigmoid(pre)
            act = pre * sig
            slope[h, rows, :] = sig * (1.0 + pre * (1.0 - sig))
            uv[h, rows, :] = act[:, :128].astype(bf16)
            b = act[:, 128:].astype(bf16)
            qk[h, rows, :] = b
            bf = b.astype(f32)
            kq[h, rows, :] = pltpu.roll(bf, 64, 1).astype(bf16)
            qz[h, rows, :] = jnp.where(lane_lo, bf * 0.125, 0.0).astype(bf16)

    n_start, n_forward, n_near, n_far = ag(0, nrm)
    g_start, g_forward, g_near, g_far = ag(1, gbuf)
    n_start()
    a2a_wait(1, recv_g)
    unpack_arrived(recv_g, gbuf, own)
    project(cx)
    n_forward()
    g_start()
    n_near()
    project(left)
    project(right)
    g_forward()
    n_far()
    project(opp)

    for j in range(2):
        for half_j in range(2):
            h = 2 * j + half_j
            for b in range(4):
                r, n = slice(b * 128, b * 128 + 128), (b + 1) * 128
                t = dot_nt(qz[h, r, :], kq[h, :n, :])
                sig = sigmoid(t)
                m = msk[r, :n]
                pw = t * sig
                p = (pw * m).astype(bf16)
                p_ref[h, r, :n] = p
                sl_ref[h, r, :n] = ((sig + pw * (1.0 - sig)) * (m * 0.125)).astype(bf16)
                pv = dot(p, uv[h, :n, :]).astype(bf16).astype(f32)
                u_here = uv[h, r, :].astype(f32)
                if half_j == 0:
                    attn_ref[r, j * 128:j * 128 + 128] = pltpu.roll(pv, 64, 1)
                    u_ref[r, j * 128:j * 128 + 128] = u_here
                else:
                    attn_ref[r, j * 128:j * 128 + 128] = jnp.where(lane_lo, attn_ref[r, j * 128:j * 128 + 128], pv)
                    u_ref[r, j * 128:j * 128 + 128] = jnp.where(
                        lane_lo, u_ref[r, j * 128:j * 128 + 128], pltpu.roll(u_here, 64, 1)
                    )

    g_near()
    g_far()
    wo_mine = pl.ds(al(cx, 256), 256)

    @pl.loop(0, 4)
    def _(b):
        r = pl.ds(al(b, 128), 128)
        dg = dot_nt(gbuf[r, :], wo[wo_mine, :])
        dg_ref[r, :] = dg
        a = attn_ref[r, :]
        m = jnp.mean(a, axis=1, keepdims=True)
        ac = a - m
        e = dg * u_ref[r, :]
        lane = iota((128, 128), 1)
        st = jnp.where(lane == 0, m, jnp.sum(ac * ac, axis=1, keepdims=True))
        st = jnp.where(lane == 2, jnp.sum(e, axis=1, keepdims=True), st)
        st = jnp.where(lane == 3, jnp.sum(e * ac, axis=1, keepdims=True), st)
        st_all[cx, :, pl.ds(al(b, 128), 128)] = jnp.transpose(st)[:8]

    for o in range(1, 4):
        rc(st_all.at[cx], st_all.at[cx], st_s, st_r, {"ctx": lax.rem(cx + o, 4)}).start()
    sends.append(lambda: wait_bytes(st_all.at[pl.ds(0, 3)], st_s, st_r).wait_send())
    wait_bytes(st_all.at[pl.ds(0, 3)], st_s, st_r).wait_recv()
    ms = [st_all[l, 0:1, :] for l in range(4)]
    m2 = (ms[0] + ms[1] + ms[2] + ms[3]) * 0.25
    sq, se, seo = 0.0, 0.0, 0.0
    for l in range(4):
        d = ms[l] - m2
        sq = sq + st_all[l, 1:2, :] + 256.0 * d * d
        se = se + st_all[l, 2:3, :]
        seo = seo + st_all[l, 3:4, :] + d * st_all[l, 2:3, :]
    r2 = lax.rsqrt(sq * (1.0 / WIDTH) + EPS)
    cmb[0:1, :] = m2
    cmb[1:2, :] = r2
    cmb[2:3, :] = se * (1.0 / WIDTH)
    cmb[3:4, :] = r2 * seo * (1.0 / WIDTH)

    for b in range(4):
        r = slice(b * 128, b * 128 + 128)
        tr = jnp.transpose(cmb[:, r])
        r2c = tr[:, 1:2]
        onorm = (attn_ref[r, :] - tr[:, 0:1]) * r2c
        u, dg = u_ref[r, :], dg_ref[r, :]
        gated[r, :] = (onorm * u).astype(bf16)
        du = (dg * onorm).astype(bf16).astype(f32)
        da = r2c * (dg * u - tr[:, 2:3] - onorm * tr[:, 3:4])
        for j in range(2):
            s = slice(j * 128, j * 128 + 128)
            dout[2 * j, r, :] = jnp.where(lane_lo, 0.0, pltpu.roll(da[:, s], 64, 1)).astype(bf16)
            dout[2 * j + 1, r, :] = jnp.where(lane_lo, 0.0, da[:, s]).astype(bf16)
            du_ref[2 * j, r, :] = du[:, s]
            du_ref[2 * j + 1, r, :] = pltpu.roll(du[:, s], 64, 1)

    for o in (2, 1, 3):
        t = lax.rem(cx + o, 4)
        rc(gated.at[pl.ds(al(t, 128), 128)], gfull.at[own], gt_s, gt_r, {"ctx": t}).start()
    sends.append(lambda: wait_bytes(gated.at[pl.ds(0, 384)], gt_s, gt_r).wait_send())
    gfull[own, :] = gated[own, :]

    half_rows = 512
    unit_rows = half_rows // n_chip

    def ar1(p):
        c = rc(ar_src.at[p, pl.ds(al(other, half_rows), half_rows)], ar_c.at[p], s1_s.at[p], s1_r.at[p], {"dp": chip * 2 + other})
        c.start()
        sends.append(c.wait_send)

    def ar2(p):
        wait_bytes(ar_c.at[p], s1_s.at[p], s1_r.at[p]).wait_recv()
        mine = pl.ds(al(chip, unit_rows), unit_rows)

        @pl.loop(0, 4)
        def _(b):
            r = pl.ds(al(b, 128), 128)
            a = ar_src[p, pl.ds(pl.multiple_of(core * half_rows + b * 128, 128), 128), :].astype(f32)
            ar_h[p, r, :] = (a + ar_c[p, r, :].astype(f32)).astype(bf16)

        ar_r[p, mine, :] = ar_h[p, mine, :]

        @pl.loop(1, n_chip)
        def _(o):
            t = lax.rem(chip + o, n_chip)
            rc(ar_h.at[p, pl.ds(al(t, unit_rows), unit_rows)], ar_r.at[p, mine], s2_s.at[p], s2_r.at[p], {"dp": t * 2 + core}).start()

        sends.append(lambda: wait_bytes(ar_h.at[p, pl.ds(0, unit_rows * (n_chip - 1))], s2_s.at[p], s2_r.at[p]).wait_send())

    def ar3(p):
        part = ar_r.at[p, pl.ds(0, unit_rows * (n_chip - 1))]
        wait_bytes(part, s2_s.at[p], s2_r.at[p]).wait_recv()
        acc = jnp.zeros((unit_rows, 256), f32)
        for k in range(n_chip):
            acc = acc + ar_r[p, k * unit_rows:(k + 1) * unit_rows, :].astype(f32)
        mine = pl.ds(pl.multiple_of(core * half_rows + chip * unit_rows, unit_rows), unit_rows)
        ar_f[p, mine, :] = acc.astype(bf16)
        ref = ar_f.at[p, mine]

        @pl.loop(1, n_chip)
        def _(o):
            rc(ref, ref, s3_s.at[p], s3_r.at[p], {"dp": lax.rem(chip + o, n_chip) * 2 + core}).start()

        sends.append(lambda: wait_bytes(part, s3_s.at[p], s3_r.at[p]).wait_send())

    def ar4(p):
        wait_bytes(ar_f.at[p, pl.ds(0, unit_rows * (n_chip - 1))], s3_s.at[p], s3_r.at[p]).wait_recv()
        ref = ar_f.at[p, pl.ds(al(core, half_rows), half_rows)]
        c = rc(ref, ref, s4_s.at[p], s4_r.at[p], {"dp": chip * 2 + other})
        c.start()
        sends.append(c.wait_send)

    def ar5(p):
        ref = ar_f.at[p, pl.ds(al(other, half_rows), half_rows)]
        wait_bytes(ref, s4_s.at[p], s4_r.at[p]).wait_recv()

    for cb in range(4):
        ar_src[0, cb * 256:cb * 256 + 256, :] = dot_tn(gated[...], gbuf[:, cb * 256:cb * 256 + 256]).astype(bf16)
    ar1(0)

    wait_bytes(gfull.at[pl.ds(0, 384)], gt_s, gt_r).wait_recv()
    for cb in range(4):
        s = slice(cb * 256, cb * 256 + 256)
        acc = xp[:, s].astype(f32)
        for c in range(4):
            acc = acc + dot(gfull[c * 128:c * 128 + 128, :], wo[c * 256:c * 256 + 256, s])
        yd[:, s] = acc.astype(bf16)
    pack_back(yd, send_y)
    a2a_start(2, send_y, recv_y)

    def backward(h):
        for b in range(4):
            r, n = slice(b * 128, b * 128 + 128), (b + 1) * 128
            dw = dot_nt(dout[h, r, :], uv[h, :n, :])
            ds = (dw * sl_ref[h, r, :n].astype(f32)).astype(bf16)
            ds_ref[r, :n] = ds
            dq_ref[r, :] = dot(ds, qk[h, :n, :])
        for b in range(4):
            r, c = slice(b * 128, b * 128 + 128), slice(b * 128, 512)
            dv = dot_tn(p_ref[h, c, r], dout[h, c, :])
            dk = dot_tn(ds_ref[c, r], qk[h, c, :])
            d1 = jnp.where(lane_lo, du_ref[h, r, :], dv)
            d2 = pltpu.roll(jnp.where(lane_lo, dk, dq_ref[r, :]), 64, 1)
            dpre[h, r, 0:128] = (d1 * slope[h, r, 0:128]).astype(bf16)
            dpre[h, r, 128:256] = (d2 * slope[h, r, 128:256]).astype(bf16)

    def piece(h):
        @pl.loop(0, 4)
        def _(q):
            acc = jnp.zeros((256, 256), f32)
            for b in range(4):
                acc = acc + dot(nrm_t[b, pl.ds(al(q, 256), 256), :], dpre[h, b * 128:b * 128 + 128, :])
            ar_src[h + 1, pl.ds(al(q, 256), 256), :] = acc.astype(bf16)

        ar1(h + 1)

    backward(0)
    piece(0)
    ar2(0)
    backward(1)
    piece(1)
    ar2(1)
    ar3(0)
    backward(2)
    piece(2)
    ar2(2)
    ar3(1)
    ar4(0)
    backward(3)

    def dnorm(block, dst):
        rows = pl.ds(al(block, 128), 128)

        @pl.loop(0, 4)
        def _(cb):
            acc = jnp.zeros((128, 256), f32)
            for h in range(4):
                acc = acc + dot_nt(dpre[h, rows, :], w[h, pl.ds(al(cb, 256), 256), :])
            dst[:, pl.ds(al(cb, 256), 256)] = acc.astype(dst.dtype)

    lo, hi = pl.ds(0, 64), pl.ds(64, 64)

    def rs_go(src, dst, k, way):
        c = rc(src, dst, rs_s.at[k], rs_r.at[k], {"ctx": way})
        c.start()
        sends.append(c.wait_send)

    def rs_wait(dst, k):
        wait_bytes(dst, rs_s.at[k], rs_r.at[k]).wait_recv()

    to_far, to_right, to_left = rs_send.at[0], rs_send.at[1], rs_send.at[2]
    dnorm(opp, to_far)
    rs_go(to_far.at[lo], rs1.at[0], 0, right)
    rs_go(to_far.at[hi], rs1.at[1], 1, left)
    dnorm(right, to_right)
    rs_go(to_right.at[hi], rs2.at[0, hi], 2, right)
    dnorm(left, to_left)
    rs_go(to_left.at[lo], rs2.at[1, lo], 3, left)
    piece(3)
    dnorm(cx, rs_own)
    rs_wait(rs1.at[0], 0)
    to_right[lo, :] = (to_right[lo, :].astype(f32) + rs1[0].astype(f32)).astype(bf16)
    rs_go(to_right.at[lo], rs2.at[0, lo], 4, right)
    rs_wait(rs1.at[1], 1)
    to_left[hi, :] = (to_left[hi, :].astype(f32) + rs1[1].astype(f32)).astype(bf16)
    rs_go(to_left.at[hi], rs2.at[1, hi], 5, left)
    ar2(3)
    ar3(2)
    ar4(1)
    ar2(4)
    ar3(3)
    ar4(2)
    a2a_wait(2, recv_y)
    unpack_home(recv_y, y_out)
    rs_wait(rs2.at[0, hi], 2)
    rs_wait(rs2.at[1, lo], 3)
    rs_wait(rs2.at[0, lo], 4)
    rs_wait(rs2.at[1, hi], 5)
    dn = rs_own[...] + rs2[0].astype(f32) + rs2[1].astype(f32)
    xh2 = xhat[...]
    mean_d = jnp.mean(dn, axis=1, keepdims=True)
    mean_dx = jnp.mean(dn * xh2, axis=1, keepdims=True)
    dx = gbuf[own, :].astype(f32) + rstd_ref[:, 0:1] * (dn - mean_d - xh2 * mean_dx)
    yd[...] = dx.astype(bf16)
    pack_back(yd, send_d)
    a2a_start(3, send_d, recv_d)
    ar3(4)
    ar4(3)
    ar4(4)
    a2a_wait(3, recv_d)
    unpack_home(recv_d, dx_out)
    for p in range(PIECES):
        ar5(p)
    finish()


def shards(stop, tokens, cotangent, packed_pos, segment_ids, w_proj, w_out):
    n_dp = lax.axis_size("dp")
    vmem, sem = pltpu.VMEM, pltpu.SemaphoreType.DMA
    scratch = [
        vmem((512, 512), bf16), vmem((512, 512), bf16),
        vmem((512, 384), bf16), vmem((512, 384), bf16),
        vmem((512, 384), bf16), vmem((512, 384), bf16),
        vmem((512, 384), bf16), vmem((512, 384), bf16),
        vmem((8, 512), f32), vmem((128, 128), i32),
        vmem((128, 1024), bf16), vmem((128, 1024), f32), vmem((128, 128), f32),
        vmem((512, 1024), bf16), vmem((4, 1024, 128), bf16), vmem((512, 1024), bf16),
        vmem((512, 512), f32), vmem((4, 512, 256), f32),
        vmem((4, 512, 128), bf16), vmem((4, 512, 128), bf16),
        vmem((4, 512, 128), bf16), vmem((4, 512, 128), bf16),
        vmem((4, 512, 512), bf16), vmem((4, 512, 512), bf16),
        vmem((512, 512), bf16), vmem((512, 128), f32),
        vmem((512, 256), f32), vmem((512, 256), f32), vmem((512, 256), f32),
        vmem((4, 8, 512), f32), vmem((128, 512), f32),
        vmem((512, 256), bf16), vmem((512, 256), bf16),
        vmem((4, 512, 128), bf16), vmem((4, 512, 128), f32), vmem((4, 512, 256), bf16),
        vmem((128, 1024), bf16),
        vmem((PIECES, 1024, 256), bf16), vmem((PIECES, 512, 256), bf16),
        vmem((PIECES, 512, 256), bf16), vmem((PIECES, 512, 256), bf16),
        vmem((3, 128, 1024), bf16), vmem((128, 1024), f32),
        vmem((2, 64, 1024), bf16), vmem((2, 128, 1024), bf16),
        sem((4,)), sem((4,)), sem((2,)), sem((2, 6)), sem, sem, sem, sem,
        sem((PIECES,)), sem((PIECES,)), sem((PIECES,)), sem((PIECES,)),
        sem((PIECES,)), sem((PIECES,)), sem((PIECES,)), sem((PIECES,)), sem((6,)), sem((6,)),
    ]
    spec = pl.BlockSpec(memory_space=pltpu.VMEM)
    y, dx, ar = pl.pallas_call(
        functools.partial(kernel, n_dp, stop),
        out_shape=[
            jax.ShapeDtypeStruct((ROWS, WIDTH), bf16),
            jax.ShapeDtypeStruct((ROWS, WIDTH), bf16),
            jax.ShapeDtypeStruct((PIECES, 1024, 256), bf16),
        ],
        in_specs=[spec] * 6,
        out_specs=[spec] * 3,
        scratch_shapes=scratch,
        compiler_params=pltpu.CompilerParams(
            collective_id=0, has_side_effects=True, vmem_limit_bytes=60 * 1024 * 1024
        ),
        cost_estimate=pl.CostEstimate(flops=6 * 10**9, bytes_accessed=12 * 10**6, transcendentals=3 * 10**6),
    )(
        tokens,
        cotangent,
        packed_pos.reshape(1, ROWS),
        segment_ids,
        jnp.transpose(w_proj, (1, 0, 2)),
        w_out,
    )
    scale = (ROWS * 4 * n_dp) ** (-0.5)
    proj = jnp.transpose(ar[1:], (1, 0, 2)).astype(f32) * scale
    out = jnp.transpose(ar[0].reshape(4, 256, 256), (1, 0, 2)).reshape(256, WIDTH).astype(f32) * scale
    return y, dx, proj, out


def solution(mesh, stop=99):
    return jax.shard_map(
        functools.partial(shards, stop),
        mesh=mesh,
        in_specs=(
            P(("dp", "ctx"), None),
            P(("dp", "ctx"), None),
            P(("dp", "ctx")),
            P("dp", None),
            P(None, "ctx", None),
            P(),
        ),
        out_specs=(
            P(("dp", "ctx"), None),
            P(("dp", "ctx"), None),
            P(None, "ctx", None),
            P("ctx", None),
        ),
        check_vma=False,
    )
```

time: 468 us -> 118 us (0.25)
  waiting for transfers between devices: 298 us -> 0 us
  Pallas kernels: 0 us -> 105 us
  starting transfers between devices: 46.9 us -> 0 us
  local copies, waits for them, and re-layouts: 49.5 us -> 10.4 us
  matrix products: 33.2 us -> 0 us
  other arithmetic: 24 us -> 1.61 us
  between operations: 14.2 us -> 0.68 us
    psum x2 -> x0, waiting for transfers between devices: 236 us -> none  [the longest x1 150 us: shards(): lax.psum(jnp.dot(gated.T, packed_g, preferred_element_type=jnp.float32),...]
    pallas_call x0 -> x1, Pallas kernels: none -> 105 us  [shards(): pl.pallas_call(functools.partial(kernel, n_dp, stop), out_shape=[jax.Shap...]
    all_to_all x9 -> x0, starting transfers between devices: 46.7 us -> none  [the longest x1 9.6 us: shards(): lax.all_to_all(send_rows, 'dp', split_axis=0, concat_axis=0, tiled=True)]
    all_to_all x9 -> x0, waiting for transfers between devices: 35.1 us -> none  [the longest x1 12.6 us: shards(): lax.all_to_all(outgoing(dx_packed), 'dp', split_axis=0, concat_axis=0, ti...]
    dot_general x12 -> x0, matrix products: 33.2 us -> none  [the longest x1 4.99 us: shards(): pre = jnp.dot(whole_normed, w_local, preferred_element_type=jnp.float32)]
    reduce_scatter x1 -> x0, waiting for transfers between devices: 18.7 us -> none  [shards(): lax.psum_scatter(jnp.dot(d_pre, w_local.T, preferred_element_type=jnp.flo...]
    all_to_all x15 -> x0, local copies, waits for them, and re-layouts: 9.27 us -> none  [the longest x2 2.12 us: shards(): lax.all_to_all(send_g, 'dp', split_axis=0, concat_axis=0, tiled=True)]
    convert_element_type x8 -> x0, other arithmetic: 9.12 us -> none  [the longest x1 3.11 us: shards(): (d_act.reshape(group, heads_dev * 4 * head_size) * silu_slope(pre)).astyp...]
  transfers between devices with their start and end apart: 13 -> 0, of which waited for: 10 -> 0; matrix products, arithmetic and copies ran while one was open for 15% -> 0% of each run, Pallas kernels for 0% -> 0%
where the time goes in v1:
time: 118 us
  Pallas kernels  105 us (89%)
  local copies, waits for them, and re-layouts  10.4 us (9%)
  other arithmetic  1.61 us (1%)
    pallas_call x1, Pallas kernels, shards(): pl.pallas_call(functools.partial(kernel, n_dp, stop), out_shape=[jax.Shap...  105 us
    unnamed x10, local copies, waits for them, and re-layouts  9.31 us

profile of v1, /device:TPU:1, one launch (start us, length us, event | category | flops | bytes accessed | tf_op | source)
XLA Modules:
  0.0 117.5 jit_solution(4914631895885382904)
XLA Ops:
  0.6 3.2 %copy.15 = bf16[1024,4,256]{2,0,1:T(8,128)(2,1)} copy(bf16[1024,4,256]{2,1,0:T(4,128)(2,1)} %param.10) | data formatting | bytes 4194304 | tf_op args[4]
  3.8 104.8 %shard_map.93 = (bf16[128,1024]{1,0:T(8,128)(2,1)}, bf16[128,1024]{1,0:T(8,128)(2,1)}, bf16[5,1024,256]{2,1,0:T(8,128)(2,1)}) custom-call(bf16[128,1024]{1,0:T(8,128)(2,1)} %tok.1, bf16[128,1024]{1,0:T(8,128)(2,1)} %cot.1, s32[1,128]{1,0:T(1,128)} %bitcast.14, s32[1,512]{1,0:T(1,128)} %seg_ref.1, bf16[4,1024,256]{2,1,0:T(8,128)(2,1)} %bitcast.12, ...), custom_call_target="tpu_custom_call" | custom-call | flops 6000000000 | bytes 12000000 | tf_op jit(solution)/shard_map/pallas_call | solution.py:549
  108.6 0.0 copy-start
  108.6 1.3 %convert_multiply_fusion = f32[1,1024,256]{2,1,0:T(8,128)S(1)} fusion(bf16[5,1024,256]{2,1,0:T(8,128)(2,1)} %get-tuple-element.9), kind=kLoop, calls=%fused_computation.2 | loop fusion | flops 524288 | bytes 1572864 | tf_op jit(solution)/shard_map/mul | solution.py:573
  109.9 1.1 copy.13
  111.0 0.0 copy-done
  111.0 0.3 multiply_bitcast_fusion
  111.4 0.0 copy-start.2
  111.4 0.0 copy-start.1
  111.4 4.7 %copy.12 = f32[1024,4,256]{2,1,0:T(4,128)} copy(f32[1024,4,256]{2,0,1:T(8,128)S(1)} %multiply_bitcast_fusion) | data formatting | bytes 8388608
  116.1 0.0 copy-done.2
  116.1 0.7 copy.18
  116.8 0.0 copy-done.1
  116.8 0.7 copy.19
Async XLA Ops:
  108.6 2.4 %copy-start = (bf16[5,1024,256]{2,1,0:T(8,128)(2,1)S(1)}, bf16[5,1024,256]{2,1,0:T(8,128)(2,1)}, u32[]{:S(2)}) copy-start(bf16[5,1024,256]{2,1,0:T(8,128)(2,1)} %get-tuple-element.9) | copy-start | bytes 7864324
  111.4 4.7 %copy-start.2 = (bf16[128,1024]{1,0:T(8,128)(2,1)S(1)}, bf16[128,1024]{1,0:T(8,128)(2,1)}, u32[]{:S(2)}) copy-start(bf16[128,1024]{1,0:T(8,128)(2,1)} %get-tuple-element.18) | copy-start | bytes 786436
  111.4 5.4 %copy-start.1 = (bf16[128,1024]{1,0:T(8,128)(2,1)S(1)}, bf16[128,1024]{1,0:T(8,128)(2,1)}, u32[]{:S(2)}) copy-start(bf16[128,1024]{1,0:T(8,128)(2,1)} %get-tuple-element.19) | copy-start | bytes 786436

commit v2 on v1

--- a/solution.py
+++ b/solution.py
@@ -44,22 +44,23 @@
 
 
 def kernel(
-    n_dp, stop,
-    tok, cot, pos_ref, seg_ref, w, wo,
-    y_out, dx_out, ar_f,
-    send_x, recv_x, send_g, recv_g, send_y, recv_y, send_d, recv_d,
+    n_dp,
+    tok_h, cot_h, pos_ref, seg_ref, w_h, wo_h,
+    y_out, recv_d, ar_f,
+    tok, cot, w, wo, in_s,
+    send_x, recv_x, send_g, recv_g, send_y, recv_y, send_d,
     meta_t, rank_s, xp, xhat, rstd_ref, nrm, nrm_t, gbuf,
     msk, slope, uv, qk, kq, qz, p_ref, sl_ref, ds_ref, dq_ref,
-    attn_ref, u_ref, dg_ref, st_all, cmb, gated, gfull, dout, du_ref, dpre,
+    attn_ref, u_ref, dg_ref, st_all, cmb, gated, gfull, dout, du_ref, dpre, dg_send,
     yd, ar_src, ar_c, ar_h, ar_r, rs_send, rs_own, rs1, rs2,
-    a2a_s, a2a_r, ag_s, ag_r, st_s, st_r, gt_s, gt_r, s1_s, s1_r, s2_s, s2_r, s3_s, s3_r, s4_s, s4_r, rs_s, rs_r,
+    a2a_s, a2a_r, ag_s, ag_r, st_s, st_r, gt_s, gt_r, dg_s, dg_r, s1_s, s1_r, s2_s, s2_r, s3_s, s3_r, s4_s, s4_r, rs_s, rs_r,
 ):
     me, cx = lax.axis_index("dp"), lax.axis_index("ctx")
     core, chip = lax.rem(me, 2), lax.div(me, 2)
     other = 1 - core
     n_chip = n_dp // 2
     right, left, opp = lax.rem(cx + 1, 4), lax.rem(cx + 3, 4), lax.rem(cx + 2, 4)
-    sends = []
+    sends, flight = [], {}
 
     def rc(src, dst, ss, rs, dev):
         return pltpu.make_async_remote_copy(
@@ -69,8 +70,16 @@
     def wait_bytes(ref, ss, rs):
         return rc(ref, ref, ss, rs, {"ctx": right})
 
+    def arrive(*keys):
+        for key in keys:
+            flight.pop(key)()
+
     def al(i, m):
         return pl.multiple_of(i * m, m)
+
+    loads = [pltpu.make_async_copy(a, b, in_s.at[i]) for i, (a, b) in enumerate([(tok_h, tok), (cot_h, cot), (w_h, w), (wo_h, wo)])]
+    for c in loads:
+        c.start()
 
     bar = pltpu.get_barrier_semaphore()
 
@@ -124,9 +133,8 @@
 
         part = src.at[pl.ds(0, (n_dp - 1) * SLOTS)]
         sends.append(lambda: wait_bytes(part, a2a_s.at[k], a2a_r.at[k]).wait_send())
-
-    def a2a_wait(k, dst):
-        wait_bytes(dst.at[pl.ds(0, (n_dp - 1) * SLOTS)], a2a_s.at[k], a2a_r.at[k]).wait_recv()
+        come = dst.at[pl.ds(0, (n_dp - 1) * SLOTS)]
+        flight["a2a", k] = lambda: wait_bytes(come, a2a_s.at[k], a2a_r.at[k]).wait_recv()
 
     def unpack_arrived(src, dst, rows):
         unit = iota((ROWS, 512), 1) & 15
@@ -168,9 +176,11 @@
         for f in sends:
             f()
 
+    loads[0].wait()
     pack_out(tok, send_x, True)
     pl.semaphore_wait(bar, n_dp - 1 + 3)
     a2a_start(0, send_x, recv_x)
+    loads[1].wait()
     pack_out(cot, send_g, False)
     a2a_start(1, send_g, recv_g)
 
@@ -183,7 +193,9 @@
     cmb[...] = jnp.zeros_like(cmb)
 
     own = pl.ds(al(cx, 128), 128)
-    a2a_wait(0, recv_x)
+    loads[2].wait()
+    loads[3].wait()
+    arrive(("a2a", 0))
     meta_t[...] = jnp.transpose(recv_x[:, 384:512].astype(f32))[:8]
     unpack_arrived(recv_x, xp, pl.ds(0, 128))
     xf = xp[...].astype(f32)
@@ -202,26 +214,28 @@
             ref = buf.at[half(block, h)]
             return rc(ref, ref, ag_s.at[k], ag_r.at[k, slot], {"ctx": way})
 
+        def go(block, h, way, slot, source):
+            to(block, h, way, slot).start()
+            sends.append(to(block, h, way, slot).wait_send)
+            flight["ag", k, slot] = to(source, h, way, slot).wait_recv
+
         def start():
-            to(cx, 0, right, 0).start()
-            to(cx, 1, left, 1).start()
-            to(cx, 1, right, 2).start()
-            to(cx, 0, left, 3).start()
+            go(cx, 0, right, 0, left)
+            go(cx, 1, left, 1, right)
+            go(cx, 1, right, 2, left)
+            go(cx, 0, left, 3, right)
 
         def forward():
-            to(left, 0, right, 0).wait_recv()
-            to(left, 0, right, 4).start()
-            to(right, 1, left, 1).wait_recv()
-            to(right, 1, left, 5).start()
-            sends.append(lambda: wait_bytes(buf.at[pl.ds(0, 384)], ag_s.at[k], ag_r.at[k, 0]).wait_send())
+            arrive(("ag", k, 0))
+            go(left, 0, right, 4, opp)
+            arrive(("ag", k, 1))
+            go(right, 1, left, 5, opp)
 
         def near():
-            to(left, 1, right, 2).wait_recv()
-            to(right, 0, left, 3).wait_recv()
+            arrive(("ag", k, 2), ("ag", k, 3))
 
         def far():
-            to(opp, 0, right, 4).wait_recv()
-            to(opp, 1, left, 5).wait_recv()
+            arrive(("ag", k, 4), ("ag", k, 5))
 
         return start, forward, near, far
 
@@ -248,16 +262,23 @@
     n_start, n_forward, n_near, n_far = ag(0, nrm)
     g_start, g_forward, g_near, g_far = ag(1, gbuf)
     n_start()
-    a2a_wait(1, recv_g)
+    arrive(("a2a", 1))
     unpack_arrived(recv_g, gbuf, own)
+    n_forward()
+    for t in range(4):
+        dg_send[t] = dot_nt(gbuf[own, :], wo[t * 256:t * 256 + 256, :]).astype(bf16)
+    for o in (2, 1, 3):
+        t = lax.rem(cx + o, 4)
+        rc(dg_send.at[t], dg_ref.at[own], dg_s, dg_r, {"ctx": t}).start()
+    sends.append(lambda: wait_bytes(dg_ref.at[pl.ds(0, 384)], dg_s, dg_r).wait_send())
+    flight["dg"] = lambda: wait_bytes(dg_ref.at[pl.ds(0, 384)], dg_s, dg_r).wait_recv()
+    dg_ref[own, :] = dg_send[cx]
     project(cx)
-    n_forward()
-    g_start()
     n_near()
     project(left)
     project(right)
-    g_forward()
     n_far()
+    g_start()
     project(opp)
 
     for j in range(2):
@@ -283,15 +304,13 @@
                         lane_lo, u_ref[r, j * 128:j * 128 + 128], pltpu.roll(u_here, 64, 1)
                     )
 
-    g_near()
-    g_far()
-    wo_mine = pl.ds(al(cx, 256), 256)
+    g_forward()
+    arrive("dg")
 
     @pl.loop(0, 4)
     def _(b):
         r = pl.ds(al(b, 128), 128)
-        dg = dot_nt(gbuf[r, :], wo[wo_mine, :])
-        dg_ref[r, :] = dg
+        dg = dg_ref[r, :].astype(f32)
         a = attn_ref[r, :]
         m = jnp.mean(a, axis=1, keepdims=True)
         ac = a - m
@@ -305,7 +324,8 @@
     for o in range(1, 4):
         rc(st_all.at[cx], st_all.at[cx], st_s, st_r, {"ctx": lax.rem(cx + o, 4)}).start()
     sends.append(lambda: wait_bytes(st_all.at[pl.ds(0, 3)], st_s, st_r).wait_send())
-    wait_bytes(st_all.at[pl.ds(0, 3)], st_s, st_r).wait_recv()
+    flight["st"] = lambda: wait_bytes(st_all.at[pl.ds(0, 3)], st_s, st_r).wait_recv()
+    arrive("st")
     ms = [st_all[l, 0:1, :] for l in range(4)]
     m2 = (ms[0] + ms[1] + ms[2] + ms[3]) * 0.25
     sq, se, seo = 0.0, 0.0, 0.0
@@ -325,7 +345,7 @@
         tr = jnp.transpose(cmb[:, r])
         r2c = tr[:, 1:2]
         onorm = (attn_ref[r, :] - tr[:, 0:1]) * r2c
-        u, dg = u_ref[r, :], dg_ref[r, :]
+        u, dg = u_ref[r, :], dg_ref[r, :].astype(f32)
         gated[r, :] = (onorm * u).astype(bf16)
         du = (dg * onorm).astype(bf16).astype(f32)
         da = r2c * (dg * u - tr[:, 2:3] - onorm * tr[:, 3:4])
@@ -340,6 +360,7 @@
         t = lax.rem(cx + o, 4)
         rc(gated.at[pl.ds(al(t, 128), 128)], gfull.at[own], gt_s, gt_r, {"ctx": t}).start()
     sends.append(lambda: wait_bytes(gated.at[pl.ds(0, 384)], gt_s, gt_r).wait_send())
+    flight["gt"] = lambda: wait_bytes(gfull.at[pl.ds(0, 384)], gt_s, gt_r).wait_recv()
     gfull[own, :] = gated[own, :]
 
     half_rows = 512
@@ -349,9 +370,10 @@
         c = rc(ar_src.at[p, pl.ds(al(other, half_rows), half_rows)], ar_c.at[p], s1_s.at[p], s1_r.at[p], {"dp": chip * 2 + other})
         c.start()
         sends.append(c.wait_send)
+        flight["s1", p] = lambda: wait_bytes(ar_c.at[p], s1_s.at[p], s1_r.at[p]).wait_recv()
 
     def ar2(p):
-        wait_bytes(ar_c.at[p], s1_s.at[p], s1_r.at[p]).wait_recv()
+        arrive(("s1", p))
         mine = pl.ds(al(chip, unit_rows), unit_rows)
 
         @pl.loop(0, 4)
@@ -368,10 +390,11 @@
             rc(ar_h.at[p, pl.ds(al(t, unit_rows), unit_rows)], ar_r.at[p, mine], s2_s.at[p], s2_r.at[p], {"dp": t * 2 + core}).start()
 
         sends.append(lambda: wait_bytes(ar_h.at[p, pl.ds(0, unit_rows * (n_chip - 1))], s2_s.at[p], s2_r.at[p]).wait_send())
+        part = ar_r.at[p, pl.ds(0, unit_rows * (n_chip - 1))]
+        flight["s2", p] = lambda: wait_bytes(part, s2_s.at[p], s2_r.at[p]).wait_recv()
 
     def ar3(p):
-        part = ar_r.at[p, pl.ds(0, unit_rows * (n_chip - 1))]
-        wait_bytes(part, s2_s.at[p], s2_r.at[p]).wait_recv()
+        arrive(("s2", p))
         acc = jnp.zeros((unit_rows, 256), f32)
         for k in range(n_chip):
             acc = acc + ar_r[p, k * unit_rows:(k + 1) * unit_rows, :].astype(f32)
@@ -383,32 +406,20 @@
         def _(o):
             rc(ref, ref, s3_s.at[p], s3_r.at[p], {"dp": lax.rem(chip + o, n_chip) * 2 + core}).start()
 
+        part = ar_f.at[p, pl.ds(0, unit_rows * (n_chip - 1))]
         sends.append(lambda: wait_bytes(part, s3_s.at[p], s3_r.at[p]).wait_send())
+        flight["s3", p] = lambda: wait_bytes(part, s3_s.at[p], s3_r.at[p]).wait_recv()
 
     def ar4(p):
-        wait_bytes(ar_f.at[p, pl.ds(0, unit_rows * (n_chip - 1))], s3_s.at[p], s3_r.at[p]).wait_recv()
+        arrive(("s3", p))
         ref = ar_f.at[p, pl.ds(al(core, half_rows), half_rows)]
         c = rc(ref, ref, s4_s.at[p], s4_r.at[p], {"dp": chip * 2 + other})
         c.start()
         sends.append(c.wait_send)
+        flight["s4", p] = lambda: wait_bytes(ref, s4_s.at[p], s4_r.at[p]).wait_recv()
 
     def ar5(p):
-        ref = ar_f.at[p, pl.ds(al(other, half_rows), half_rows)]
-        wait_bytes(ref, s4_s.at[p], s4_r.at[p]).wait_recv()
-
-    for cb in range(4):
-        ar_src[0, cb * 256:cb * 256 + 256, :] = dot_tn(gated[...], gbuf[:, cb * 256:cb * 256 + 256]).astype(bf16)
-    ar1(0)
-
-    wait_bytes(gfull.at[pl.ds(0, 384)], gt_s, gt_r).wait_recv()
-    for cb in range(4):
-        s = slice(cb * 256, cb * 256 + 256)
-        acc = xp[:, s].astype(f32)
-        for c in range(4):
-            acc = acc + dot(gfull[c * 128:c * 128 + 128, :], wo[c * 256:c * 256 + 256, s])
-        yd[:, s] = acc.astype(bf16)
-    pack_back(yd, send_y)
-    a2a_start(2, send_y, recv_y)
+        arrive(("s4", p))
 
     def backward(h):
         for b in range(4):
@@ -436,20 +447,6 @@
 
         ar1(h + 1)
 
-    backward(0)
-    piece(0)
-    ar2(0)
-    backward(1)
-    piece(1)
-    ar2(1)
-    ar3(0)
-    backward(2)
-    piece(2)
-    ar2(2)
-    ar3(1)
-    ar4(0)
-    backward(3)
-
     def dnorm(block, dst):
         rows = pl.ds(al(block, 128), 128)
 
@@ -466,9 +463,34 @@
         c = rc(src, dst, rs_s.at[k], rs_r.at[k], {"ctx": way})
         c.start()
         sends.append(c.wait_send)
-
-    def rs_wait(dst, k):
-        wait_bytes(dst, rs_s.at[k], rs_r.at[k]).wait_recv()
+        flight["rs", k] = c.wait_recv
+
+    backward(0)
+    piece(0)
+    g_near()
+    g_far()
+    for cb in range(4):
+        ar_src[0, cb * 256:cb * 256 + 256, :] = dot_tn(gated[...], gbuf[:, cb * 256:cb * 256 + 256]).astype(bf16)
+    ar1(0)
+    backward(1)
+    piece(1)
+    ar2(1)
+    arrive("gt")
+    for cb in range(4):
+        s = slice(cb * 256, cb * 256 + 256)
+        acc = xp[:, s].astype(f32)
+        for c in range(4):
+            acc = acc + dot(gfull[c * 128:c * 128 + 128, :], wo[c * 256:c * 256 + 256, s])
+        yd[:, s] = acc.astype(bf16)
+    pack_back(yd, send_y)
+    a2a_start(2, send_y, recv_y)
+
+    ar2(0)
+    backward(2)
+    piece(2)
+    ar2(2)
+    ar3(1)
+    backward(3)
 
     to_far, to_right, to_left = rs_send.at[0], rs_send.at[1], rs_send.at[2]
     dnorm(opp, to_far)
@@ -479,25 +501,19 @@
     dnorm(left, to_left)
     rs_go(to_left.at[lo], rs2.at[1, lo], 3, left)
     piece(3)
-    dnorm(cx, rs_own)
-    rs_wait(rs1.at[0], 0)
+    ar2(3)
+    ar3(0)
+    arrive(("rs", 0))
     to_right[lo, :] = (to_right[lo, :].astype(f32) + rs1[0].astype(f32)).astype(bf16)
     rs_go(to_right.at[lo], rs2.at[0, lo], 4, right)
-    rs_wait(rs1.at[1], 1)
+    arrive(("rs", 1))
     to_left[hi, :] = (to_left[hi, :].astype(f32) + rs1[1].astype(f32)).astype(bf16)
     rs_go(to_left.at[hi], rs2.at[1, hi], 5, left)
-    ar2(3)
+    dnorm(cx, rs_own)
+    ar2(4)
     ar3(2)
     ar4(1)
-    ar2(4)
-    ar3(3)
-    ar4(2)
-    a2a_wait(2, recv_y)
-    unpack_home(recv_y, y_out)
-    rs_wait(rs2.at[0, hi], 2)
-    rs_wait(rs2.at[1, lo], 3)
-    rs_wait(rs2.at[0, lo], 4)
-    rs_wait(rs2.at[1, hi], 5)
+    arrive(("rs", 2), ("rs", 3), ("rs", 4), ("rs", 5))
     dn = rs_own[...] + rs2[0].astype(f32) + rs2[1].astype(f32)
     xh2 = xhat[...]
     mean_d = jnp.mean(dn, axis=1, keepdims=True)
@@ -506,24 +522,50 @@
     yd[...] = dx.astype(bf16)
     pack_back(yd, send_d)
     a2a_start(3, send_d, recv_d)
+    ar3(3)
+    ar4(0)
+    ar4(2)
     ar3(4)
     ar4(3)
+    arrive(("a2a", 2))
+    unpack_home(recv_y, y_out)
     ar4(4)
-    a2a_wait(3, recv_d)
-    unpack_home(recv_d, dx_out)
+    arrive(("a2a", 3))
     for p in range(PIECES):
         ar5(p)
     finish()
 
 
-def shards(stop, tokens, cotangent, packed_pos, segment_ids, w_proj, w_out):
+def last(scale, y, recv, pos_ref, ar, y_out, dx_out, proj, out):
+    c = pl.program_id(0)
+    y_out[...] = y[...]
+    pos_l = jnp.broadcast_to(pos_ref[...], (ROWS, ROWS))
+    pos_s = jnp.transpose(pos_l.astype(f32)).astype(i32)
+    tgt_l, tgt_s = lax.shift_right_logical(pos_l, 9), lax.shift_right_logical(pos_s, 9)
+    before = (tgt_l == tgt_s) & (iota((ROWS, ROWS), 1) < iota((ROWS, ROWS), 0))
+    rank = jnp.sum(jnp.where(before, 1.0, 0.0), axis=1, keepdims=True).astype(i32)
+    base = tgt_s[:, 0:1] * SLOTS
+    lanes = iota((ROWS, 512), 1)
+    acc = jnp.zeros((ROWS, 128), f32)
+    for L in range(3):
+        v = rank + (c * CAP - 16 * L)
+        idx = jnp.where((v >= 0) & (v < 16), base + v, -1)
+        acc = acc + dot(one(lanes == idx), recv[:, L * 128:L * 128 + 128])
+    dx_out[...] = acc.astype(bf16)
+    out[...] = ar[0].astype(f32) * scale
+    for h in range(4):
+        proj[:, h, :] = ar[h + 1].astype(f32) * scale
+
+
+def shards(tokens, cotangent, packed_pos, segment_ids, w_proj, w_out):
     n_dp = lax.axis_size("dp")
     vmem, sem = pltpu.VMEM, pltpu.SemaphoreType.DMA
     scratch = [
+        vmem((128, 1024), bf16), vmem((128, 1024), bf16), vmem((4, 1024, 256), bf16), vmem((1024, 1024), bf16), sem((4,)),
         vmem((512, 512), bf16), vmem((512, 512), bf16),
         vmem((512, 384), bf16), vmem((512, 384), bf16),
         vmem((512, 384), bf16), vmem((512, 384), bf16),
-        vmem((512, 384), bf16), vmem((512, 384), bf16),
+        vmem((512, 384), bf16),
         vmem((8, 512), f32), vmem((128, 128), i32),
         vmem((128, 1024), bf16), vmem((128, 1024), f32), vmem((128, 128), f32),
         vmem((512, 1024), bf16), vmem((4, 1024, 128), bf16), vmem((512, 1024), bf16),
@@ -532,51 +574,66 @@
         vmem((4, 512, 128), bf16), vmem((4, 512, 128), bf16),
         vmem((4, 512, 512), bf16), vmem((4, 512, 512), bf16),
         vmem((512, 512), bf16), vmem((512, 128), f32),
-        vmem((512, 256), f32), vmem((512, 256), f32), vmem((512, 256), f32),
+        vmem((512, 256), f32), vmem((512, 256), f32), vmem((512, 256), bf16),
         vmem((4, 8, 512), f32), vmem((128, 512), f32),
         vmem((512, 256), bf16), vmem((512, 256), bf16),
         vmem((4, 512, 128), bf16), vmem((4, 512, 128), f32), vmem((4, 512, 256), bf16),
+        vmem((4, 128, 256), bf16),
         vmem((128, 1024), bf16),
         vmem((PIECES, 1024, 256), bf16), vmem((PIECES, 512, 256), bf16),
         vmem((PIECES, 512, 256), bf16), vmem((PIECES, 512, 256), bf16),
         vmem((3, 128, 1024), bf16), vmem((128, 1024), f32),
         vmem((2, 64, 1024), bf16), vmem((2, 128, 1024), bf16),
-        sem((4,)), sem((4,)), sem((2,)), sem((2, 6)), sem, sem, sem, sem,
+        sem((4,)), sem((4,)), sem((2,)), sem((2, 6)), sem, sem, sem, sem, sem, sem,
         sem((PIECES,)), sem((PIECES,)), sem((PIECES,)), sem((PIECES,)),
         sem((PIECES,)), sem((PIECES,)), sem((PIECES,)), sem((PIECES,)), sem((6,)), sem((6,)),
     ]
-    spec = pl.BlockSpec(memory_space=pltpu.VMEM)
+    spec, free = pl.BlockSpec(memory_space=pltpu.VMEM), pl.BlockSpec(memory_space=pl.ANY)
+    pos = packed_pos.reshape(1, ROWS)
     y, dx, ar = pl.pallas_call(
-        functools.partial(kernel, n_dp, stop),
+        functools.partial(kernel, n_dp),
         out_shape=[
             jax.ShapeDtypeStruct((ROWS, WIDTH), bf16),
-            jax.ShapeDtypeStruct((ROWS, WIDTH), bf16),
+            jax.ShapeDtypeStruct((512, 384), bf16),
             jax.ShapeDtypeStruct((PIECES, 1024, 256), bf16),
         ],
-        in_specs=[spec] * 6,
+        in_specs=[free, free, spec, spec, free, free],
         out_specs=[spec] * 3,
         scratch_shapes=scratch,
         compiler_params=pltpu.CompilerParams(
             collective_id=0, has_side_effects=True, vmem_limit_bytes=60 * 1024 * 1024
         ),
         cost_estimate=pl.CostEstimate(flops=6 * 10**9, bytes_accessed=12 * 10**6, transcendentals=3 * 10**6),
-    )(
-        tokens,
-        cotangent,
-        packed_pos.reshape(1, ROWS),
-        segment_ids,
-        jnp.transpose(w_proj, (1, 0, 2)),
-        w_out,
-    )
+    )(tokens, cotangent, pos, segment_ids, jnp.transpose(w_proj, (1, 0, 2)), w_out)
     scale = (ROWS * 4 * n_dp) ** (-0.5)
-    proj = jnp.transpose(ar[1:], (1, 0, 2)).astype(f32) * scale
-    out = jnp.transpose(ar[0].reshape(4, 256, 256), (1, 0, 2)).reshape(256, WIDTH).astype(f32) * scale
-    return y, dx, proj, out
-
-
-def solution(mesh, stop=99):
+    return pl.pallas_call(
+        functools.partial(last, scale),
+        grid=(8,),
+        out_shape=[
+            jax.ShapeDtypeStruct((ROWS, WIDTH), bf16),
+            jax.ShapeDtypeStruct((ROWS, WIDTH), bf16),
+            jax.ShapeDtypeStruct((1024, 4, 256), f32),
+            jax.ShapeDtypeStruct((256, WIDTH), f32),
+        ],
+        in_specs=[
+            pl.BlockSpec((16, WIDTH), lambda i: (i, 0)),
+            pl.BlockSpec((512, 384), lambda i: (0, 0)),
+            pl.BlockSpec((1, ROWS), lambda i: (0, 0)),
+            pl.BlockSpec((PIECES, 128, 256), lambda i: (0, i, 0)),
+        ],
+        out_specs=[
+            pl.BlockSpec((16, WIDTH), lambda i: (i, 0)),
+            pl.BlockSpec((ROWS, 128), lambda i: (0, i)),
+            pl.BlockSpec((128, 4, 256), lambda i: (i, 0, 0)),
+            pl.BlockSpec((128, 256), lambda i: (i % 2, i // 2)),
+        ],
+        cost_estimate=pl.CostEstimate(flops=10**8, bytes_accessed=10 * 10**6, transcendentals=0),
+    )(y, dx, pos, ar)
+
+
+def solution(mesh):
     return jax.shard_map(
-        functools.partial(shards, stop),
+        shards,
         mesh=mesh,
         in_specs=(
             P(("dp", "ctx"), None),

time: 118 us -> 106 us (0.90)
  local copies, waits for them, and re-layouts: 10.4 us -> 3.18 us
  Pallas kernels: 105 us -> 102 us
  other arithmetic: 1.61 us -> 0 us
    unnamed x10 -> x1, local copies, waits for them, and re-layouts: 9.31 us -> 3.18 us
    pallas_call x1 -> x2, Pallas kernels: 105 us -> 102 us  [the longest x1 92.7 us: shards(): pl.pallas_call(functools.partial(kernel, n_dp), out_shape=[jax.ShapeDtype...]
    mul x2 -> x0, other arithmetic: 1.61 us -> none  [the longest x1 1.26 us: shards(): jnp.transpose(ar[0].reshape(4, 256, 256), (1, 0, 2)).reshape(256, WIDTH)]
where the time goes in v2:
time: 106 us; the launch traced here: 105 us
  Pallas kernels  102 us (96%)
  local copies, waits for them, and re-layouts  3.18 us (3%)
    pallas_call x1, Pallas kernels, shards(): pl.pallas_call(functools.partial(kernel, n_dp), out_shape=[jax.ShapeDtype...  92.7 us
    pallas_call x1, Pallas kernels, shards(): pl.pallas_call(functools.partial(last, scale), grid=(8,), out_shape=[jax....  8.86 us
    unnamed x1, local copies, waits for them, and re-layouts  3.18 us

profile of v2, /device:TPU:1, one launch (start us, length us, event | category | flops | bytes accessed | tf_op | source)
XLA Modules:
  0.0 105.4 jit_solution(14128766460058812982)
XLA Ops:
  0.6 3.2 %copy.12 = bf16[1024,4,256]{2,0,1:T(8,128)(2,1)} copy(bf16[1024,4,256]{2,1,0:T(4,128)(2,1)} %param.10) | data formatting | bytes 4194304 | tf_op args[4]
  3.8 92.7 %shard_map.93 = (bf16[128,1024]{1,0:T(8,128)(2,1)}, bf16[512,384]{1,0:T(8,128)(2,1)}, bf16[5,1024,256]{2,1,0:T(8,128)(2,1)}) custom-call(bf16[128,1024]{1,0:T(8,128)(2,1)} %tok_h.1, bf16[128,1024]{1,0:T(8,128)(2,1)} %cot_h.1, s32[1,128]{1,0:T(1,128)} %bitcast.5, s32[1,512]{1,0:T(1,128)} %seg_ref.1, bf16[4,1024,256]{2,1,0:T(8,128)(2,1)} %bitcast.4, ...), custom_call_target="tpu_custom_call" | custom-call | flops 6000000000 | bytes 12000000 | tf_op jit(solution)/shard_map/pallas_call | solution.py:593
  96.5 8.9 %shard_map.94 = (bf16[128,1024]{1,0:T(8,128)(2,1)}, bf16[128,1024]{1,0:T(8,128)(2,1)}, f32[1024,4,256]{2,1,0:T(4,128)}, f32[256,1024]{1,0:T(8,128)}) custom-call(bf16[128,1024]{1,0:T(8,128)(2,1)} %get-tuple-element.7.y, bf16[512,384]{1,0:T(8,128)(2,1)} %get-tuple-element.8.recv, s32[1,128]{1,0:T(1,128)} %bitcast.6, bf16[5,1024,256]{2,1,0:T(8,128)(2,1)} %get-tuple-element.9.ar), custom_call_target="tpu_custom_call" | custom-call | flops 100000000 | bytes 10000000 | tf_op jit(solution)/shard_map/pallas_call | solution.py:609

commit v3 on v2

--- a/solution.py
+++ b/solution.py
@@ -47,18 +47,17 @@
     n_dp,
     tok_h, cot_h, pos_ref, seg_ref, w_h, wo_h,
     y_out, recv_d, ar_f,
-    tok, cot, w, wo, in_s,
+    tok, cot, w_raw, w, wo, in_s,
     send_x, recv_x, send_g, recv_g, send_y, recv_y, send_d,
     meta_t, rank_s, xp, xhat, rstd_ref, nrm, nrm_t, gbuf,
     msk, slope, uv, qk, kq, qz, p_ref, sl_ref, ds_ref, dq_ref,
     attn_ref, u_ref, dg_ref, st_all, cmb, gated, gfull, dout, du_ref, dpre, dg_send,
-    yd, ar_src, ar_c, ar_h, ar_r, rs_send, rs_own, rs1, rs2,
-    a2a_s, a2a_r, ag_s, ag_r, st_s, st_r, gt_s, gt_r, dg_s, dg_r, s1_s, s1_r, s2_s, s2_r, s3_s, s3_r, s4_s, s4_r, rs_s, rs_r,
+    yd, ar_src, ar_c, ar_h, ar_r, ar_q, ar_b, rs_send, rs_own, rs1, rs2,
+    a2a_s, a2a_r, ag_s, ag_r, st_s, st_r, gt_s, gt_r, dg_s, dg_r, ar_ss, ar_rs, rs_s, rs_r,
 ):
     me, cx = lax.axis_index("dp"), lax.axis_index("ctx")
     core, chip = lax.rem(me, 2), lax.div(me, 2)
     other = 1 - core
-    n_chip = n_dp // 2
     right, left, opp = lax.rem(cx + 1, 4), lax.rem(cx + 3, 4), lax.rem(cx + 2, 4)
     sends, flight = [], {}
 
@@ -77,7 +76,7 @@
     def al(i, m):
         return pl.multiple_of(i * m, m)
 
-    loads = [pltpu.make_async_copy(a, b, in_s.at[i]) for i, (a, b) in enumerate([(tok_h, tok), (cot_h, cot), (w_h, w), (wo_h, wo)])]
+    loads = [pltpu.make_async_copy(a, b, in_s.at[i]) for i, (a, b) in enumerate([(tok_h, tok), (cot_h, cot), (w_h, w_raw), (wo_h, wo)])]
     for c in loads:
         c.start()
 
@@ -194,6 +193,12 @@
 
     own = pl.ds(al(cx, 128), 128)
     loads[2].wait()
+
+    @pl.loop(0, 16)
+    def _(i):
+        rows = pl.ds(al(i, 64), 64)
+        w[:, rows, :] = jnp.swapaxes(w_raw[rows].astype(f32), 0, 1).astype(bf16)
+
     loads[3].wait()
     arrive(("a2a", 0))
     meta_t[...] = jnp.transpose(recv_x[:, 384:512].astype(f32))[:8]
@@ -363,63 +368,106 @@
     flight["gt"] = lambda: wait_bytes(gfull.at[pl.ds(0, 384)], gt_s, gt_r).wait_recv()
     gfull[own, :] = gated[own, :]
 
-    half_rows = 512
-    unit_rows = half_rows // n_chip
+    yy, zz = lax.div(chip, 4), lax.rem(chip, 4)
+    base = core * 512
+
+    def rows_at(start, count):
+        return pl.ds(pl.multiple_of(start, count), count)
+
+    def peer(axis, o):
+        y2, z2 = (yy, lax.rem(zz + o, 4)) if axis == 0 else (lax.rem(yy + o, 4), zz)
+        return lax.rem((zz if axis == 0 else yy) + o, 4), {"dp": (y2 * 4 + z2) * 2 + core}
+
+    def ours(part):
+        return (zz, yy) if part == 0 else (yy, zz)
+
+    def begun(stage, p, ref):
+        sends.append(lambda: wait_bytes(ref, ar_ss.at[stage, p], ar_rs.at[stage, p]).wait_send())
+        flight["ar", stage, p] = lambda: wait_bytes(ref, ar_ss.at[stage, p], ar_rs.at[stage, p]).wait_recv()
+
+    def to_core(stage, p, src, dst):
+        rc(src, dst, ar_ss.at[stage, p], ar_rs.at[stage, p], {"dp": chip * 2 + other}).start()
+        begun(stage, p, dst)
+
+    def to_axis(stage, p, places, ref):
+        @pl.loop(1, 4)
+        def _(o):
+            for part in range(2):
+                axis = part if stage in (1, 4) else 1 - part
+                t, dev = peer(axis, o)
+                src, dst = places(part, t)
+                rc(src, dst, ar_ss.at[stage, p], ar_rs.at[stage, p], dev).start()
+
+        begun(stage, p, ref)
 
     def ar1(p):
-        c = rc(ar_src.at[p, pl.ds(al(other, half_rows), half_rows)], ar_c.at[p], s1_s.at[p], s1_r.at[p], {"dp": chip * 2 + other})
-        c.start()
-        sends.append(c.wait_send)
-        flight["s1", p] = lambda: wait_bytes(ar_c.at[p], s1_s.at[p], s1_r.at[p]).wait_recv()
+        to_core(0, p, ar_src.at[p, rows_at(other * 512, 512)], ar_c.at[p])
 
     def ar2(p):
-        arrive(("s1", p))
-        mine = pl.ds(al(chip, unit_rows), unit_rows)
+        arrive(("ar", 0, p))
 
         @pl.loop(0, 4)
         def _(b):
-            r = pl.ds(al(b, 128), 128)
-            a = ar_src[p, pl.ds(pl.multiple_of(core * half_rows + b * 128, 128), 128), :].astype(f32)
+            r = rows_at(b * 128, 128)
+            a = ar_src[p, rows_at(base + b * 128, 128), :].astype(f32)
             ar_h[p, r, :] = (a + ar_c[p, r, :].astype(f32)).astype(bf16)
 
-        ar_r[p, mine, :] = ar_h[p, mine, :]
-
-        @pl.loop(1, n_chip)
-        def _(o):
-            t = lax.rem(chip + o, n_chip)
-            rc(ar_h.at[p, pl.ds(al(t, unit_rows), unit_rows)], ar_r.at[p, mine], s2_s.at[p], s2_r.at[p], {"dp": t * 2 + core}).start()
-
-        sends.append(lambda: wait_bytes(ar_h.at[p, pl.ds(0, unit_rows * (n_chip - 1))], s2_s.at[p], s2_r.at[p]).wait_send())
-        part = ar_r.at[p, pl.ds(0, unit_rows * (n_chip - 1))]
-        flight["s2", p] = lambda: wait_bytes(part, s2_s.at[p], s2_r.at[p]).wait_recv()
+        for part in range(2):
+            mine = rows_at(part * 256 + ours(part)[0] * 64, 64)
+            ar_r[p, mine, :] = ar_h[p, mine, :]
+
+        def places(part, t):
+            return (
+                ar_h.at[p, rows_at(part * 256 + t * 64, 64)],
+                ar_r.at[p, rows_at(part * 256 + ours(part)[0] * 64, 64)],
+            )
+
+        to_axis(1, p, places, ar_r.at[p, pl.ds(0, 384)])
 
     def ar3(p):
-        arrive(("s2", p))
-        acc = jnp.zeros((unit_rows, 256), f32)
-        for k in range(n_chip):
-            acc = acc + ar_r[p, k * unit_rows:(k + 1) * unit_rows, :].astype(f32)
-        mine = pl.ds(pl.multiple_of(core * half_rows + chip * unit_rows, unit_rows), unit_rows)
-        ar_f[p, mine, :] = acc.astype(bf16)
-        ref = ar_f.at[p, mine]
-
-        @pl.loop(1, n_chip)
-        def _(o):
-            rc(ref, ref, s3_s.at[p], s3_r.at[p], {"dp": lax.rem(chip + o, n_chip) * 2 + core}).start()
-
-        part = ar_f.at[p, pl.ds(0, unit_rows * (n_chip - 1))]
-        sends.append(lambda: wait_bytes(part, s3_s.at[p], s3_r.at[p]).wait_send())
-        flight["s3", p] = lambda: wait_bytes(part, s3_s.at[p], s3_r.at[p]).wait_recv()
+        arrive(("ar", 1, p))
+        for part in range(2):
+            acc = jnp.zeros((64, 256), f32)
+            for k in range(4):
+                acc = acc + ar_r[p, part * 256 + k * 64:part * 256 + k * 64 + 64, :].astype(f32)
+            ar_q[p, part * 64:part * 64 + 64, :] = acc.astype(bf16)
+            mine = rows_at(part * 64 + ours(part)[1] * 16, 16)
+            ar_b[p, mine, :] = ar_q[p, mine, :]
+
+        def places(part, t):
+            return ar_q.at[p, rows_at(part * 64 + t * 16, 16)], ar_b.at[p, rows_at(part * 64 + ours(part)[1] * 16, 16)]
+
+        to_axis(2, p, places, ar_b.at[p, pl.ds(0, 96)])
 
     def ar4(p):
-        arrive(("s3", p))
-        ref = ar_f.at[p, pl.ds(al(core, half_rows), half_rows)]
-        c = rc(ref, ref, s4_s.at[p], s4_r.at[p], {"dp": chip * 2 + other})
-        c.start()
-        sends.append(c.wait_send)
-        flight["s4", p] = lambda: wait_bytes(ref, s4_s.at[p], s4_r.at[p]).wait_recv()
+        arrive(("ar", 2, p))
+        for part in range(2):
+            acc = jnp.zeros((16, 256), f32)
+            for k in range(4):
+                acc = acc + ar_b[p, part * 64 + k * 16:part * 64 + k * 16 + 16, :].astype(f32)
+            first, second = ours(part)
+            ar_f[p, rows_at(base + part * 256 + first * 64 + second * 16, 16), :] = acc.astype(bf16)
+
+        def places(part, t):
+            first, second = ours(part)
+            ref = ar_f.at[p, rows_at(base + part * 256 + first * 64 + second * 16, 16)]
+            return ref, ref
+
+        to_axis(3, p, places, ar_f.at[p, pl.ds(0, 96)])
 
     def ar5(p):
-        arrive(("s4", p))
+        arrive(("ar", 3, p))
+
+        def places(part, t):
+            ref = ar_f.at[p, rows_at(base + part * 256 + ours(part)[0] * 64, 64)]
+            return ref, ref
+
+        to_axis(4, p, places, ar_f.at[p, pl.ds(0, 384)])
+
+    def ar6(p):
+        arrive(("ar", 4, p))
+        ref = ar_f.at[p, rows_at(base, 512)]
+        to_core(5, p, ref, ref)
 
     def backward(h):
         for b in range(4):
@@ -486,10 +534,12 @@
     a2a_start(2, send_y, recv_y)
 
     ar2(0)
+    ar3(1)
     backward(2)
     piece(2)
     ar2(2)
-    ar3(1)
+    ar3(0)
+    ar4(1)
     backward(3)
 
     to_far, to_right, to_left = rs_send.at[0], rs_send.at[1], rs_send.at[2]
@@ -502,17 +552,25 @@
     rs_go(to_left.at[lo], rs2.at[1, lo], 3, left)
     piece(3)
     ar2(3)
-    ar3(0)
+    ar3(2)
+    ar4(0)
+    ar5(1)
     arrive(("rs", 0))
     to_right[lo, :] = (to_right[lo, :].astype(f32) + rs1[0].astype(f32)).astype(bf16)
     rs_go(to_right.at[lo], rs2.at[0, lo], 4, right)
     arrive(("rs", 1))
     to_left[hi, :] = (to_left[hi, :].astype(f32) + rs1[1].astype(f32)).astype(bf16)
     rs_go(to_left.at[hi], rs2.at[1, hi], 5, left)
+    ar2(4)
+    ar3(3)
+    ar4(2)
+    ar5(0)
+    ar6(1)
     dnorm(cx, rs_own)
-    ar2(4)
-    ar3(2)
-    ar4(1)
+    ar3(4)
+    ar4(3)
+    ar5(2)
+    ar6(0)
     arrive(("rs", 2), ("rs", 3), ("rs", 4), ("rs", 5))
     dn = rs_own[...] + rs2[0].astype(f32) + rs2[1].astype(f32)
     xh2 = xhat[...]
@@ -522,22 +580,22 @@
     yd[...] = dx.astype(bf16)
     pack_back(yd, send_d)
     a2a_start(3, send_d, recv_d)
-    ar3(3)
-    ar4(0)
-    ar4(2)
-    ar3(4)
-    ar4(3)
+    ar4(4)
+    ar5(3)
+    ar6(2)
     arrive(("a2a", 2))
     unpack_home(recv_y, y_out)
-    ar4(4)
+    ar5(4)
+    ar6(3)
+    ar6(4)
     arrive(("a2a", 3))
     for p in range(PIECES):
-        ar5(p)
+        arrive(("ar", 5, p))
     finish()
 
 
 def last(scale, y, recv, pos_ref, ar, y_out, dx_out, proj, out):
-    c = pl.program_id(0)
+    i = pl.program_id(0)
     y_out[...] = y[...]
     pos_l = jnp.broadcast_to(pos_ref[...], (ROWS, ROWS))
     pos_s = jnp.transpose(pos_l.astype(f32)).astype(i32)
@@ -546,22 +604,25 @@
     rank = jnp.sum(jnp.where(before, 1.0, 0.0), axis=1, keepdims=True).astype(i32)
     base = tgt_s[:, 0:1] * SLOTS
     lanes = iota((ROWS, 512), 1)
-    acc = jnp.zeros((ROWS, 128), f32)
-    for L in range(3):
-        v = rank + (c * CAP - 16 * L)
-        idx = jnp.where((v >= 0) & (v < 16), base + v, -1)
-        acc = acc + dot(one(lanes == idx), recv[:, L * 128:L * 128 + 128])
-    dx_out[...] = acc.astype(bf16)
+    for k in range(2):
+        acc = jnp.zeros((ROWS, 128), f32)
+        for L in range(3):
+            v = rank + ((2 * i + k) * CAP - 16 * L)
+            idx = jnp.where((v >= 0) & (v < 16), base + v, -1)
+            acc = acc + dot(one(lanes == idx), recv[:, L * 128:L * 128 + 128])
+        dx_out[:, k * 128:k * 128 + 128] = acc.astype(bf16)
     out[...] = ar[0].astype(f32) * scale
-    for h in range(4):
-        proj[:, h, :] = ar[h + 1].astype(f32) * scale
+    for q in range(8):
+        r = slice(q * 32, q * 32 + 32)
+        proj[r] = jnp.swapaxes(ar[1:, r, :].astype(f32) * scale, 0, 1)
 
 
 def shards(tokens, cotangent, packed_pos, segment_ids, w_proj, w_out):
     n_dp = lax.axis_size("dp")
     vmem, sem = pltpu.VMEM, pltpu.SemaphoreType.DMA
     scratch = [
-        vmem((128, 1024), bf16), vmem((128, 1024), bf16), vmem((4, 1024, 256), bf16), vmem((1024, 1024), bf16), sem((4,)),
+        vmem((128, 1024), bf16), vmem((128, 1024), bf16), vmem((1024, 4, 256), bf16), vmem((4, 1024, 256), bf16),
+        vmem((1024, 1024), bf16), sem((4,)),
         vmem((512, 512), bf16), vmem((512, 512), bf16),
         vmem((512, 384), bf16), vmem((512, 384), bf16),
         vmem((512, 384), bf16), vmem((512, 384), bf16),
@@ -582,11 +643,11 @@
         vmem((128, 1024), bf16),
         vmem((PIECES, 1024, 256), bf16), vmem((PIECES, 512, 256), bf16),
         vmem((PIECES, 512, 256), bf16), vmem((PIECES, 512, 256), bf16),
+        vmem((PIECES, 128, 256), bf16), vmem((PIECES, 128, 256), bf16),
         vmem((3, 128, 1024), bf16), vmem((128, 1024), f32),
         vmem((2, 64, 1024), bf16), vmem((2, 128, 1024), bf16),
         sem((4,)), sem((4,)), sem((2,)), sem((2, 6)), sem, sem, sem, sem, sem, sem,
-        sem((PIECES,)), sem((PIECES,)), sem((PIECES,)), sem((PIECES,)),
-        sem((PIECES,)), sem((PIECES,)), sem((PIECES,)), sem((PIECES,)), sem((6,)), sem((6,)),
+        sem((6, PIECES)), sem((6, PIECES)), sem((6,)), sem((6,)),
     ]
     spec, free = pl.BlockSpec(memory_space=pltpu.VMEM), pl.BlockSpec(memory_space=pl.ANY)
     pos = packed_pos.reshape(1, ROWS)
@@ -604,11 +665,11 @@
             collective_id=0, has_side_effects=True, vmem_limit_bytes=60 * 1024 * 1024
         ),
         cost_estimate=pl.CostEstimate(flops=6 * 10**9, bytes_accessed=12 * 10**6, transcendentals=3 * 10**6),
-    )(tokens, cotangent, pos, segment_ids, jnp.transpose(w_proj, (1, 0, 2)), w_out)
+    )(tokens, cotangent, pos, segment_ids, w_proj, w_out)
     scale = (ROWS * 4 * n_dp) ** (-0.5)
     return pl.pallas_call(
         functools.partial(last, scale),
-        grid=(8,),
+        grid=(4,),
         out_shape=[
             jax.ShapeDtypeStruct((ROWS, WIDTH), bf16),
             jax.ShapeDtypeStruct((ROWS, WIDTH), bf16),
@@ -616,17 +677,18 @@
             jax.ShapeDtypeStruct((256, WIDTH), f32),
         ],
         in_specs=[
-            pl.BlockSpec((16, WIDTH), lambda i: (i, 0)),
+            pl.BlockSpec((32, WIDTH), lambda i: (i, 0)),
             pl.BlockSpec((512, 384), lambda i: (0, 0)),
             pl.BlockSpec((1, ROWS), lambda i: (0, 0)),
-            pl.BlockSpec((PIECES, 128, 256), lambda i: (0, i, 0)),
+            pl.BlockSpec((PIECES, 256, 256), lambda i: (0, i, 0)),
         ],
         out_specs=[
-            pl.BlockSpec((16, WIDTH), lambda i: (i, 0)),
-            pl.BlockSpec((ROWS, 128), lambda i: (0, i)),
-            pl.BlockSpec((128, 4, 256), lambda i: (i, 0, 0)),
-            pl.BlockSpec((128, 256), lambda i: (i % 2, i // 2)),
+            pl.BlockSpec((32, WIDTH), lambda i: (i, 0)),
+            pl.BlockSpec((ROWS, 256), lambda i: (0, i)),
+            pl.BlockSpec((256, 4, 256), lambda i: (i, 0, 0)),
+            pl.BlockSpec((256, 256), lambda i: (0, i)),
         ],
+        compiler_params=pltpu.CompilerParams(vmem_limit_bytes=40 * 1024 * 1024),
         cost_estimate=pl.CostEstimate(flops=10**8, bytes_accessed=10 * 10**6, transcendentals=0),
     )(y, dx, pos, ar)
 

time: 106 us -> 103 us (0.972)
  Pallas kernels: 102 us -> 98.1 us
    pallas_call x1, Pallas kernels: 8.86 us -> 4.57 us  [shards(): pl.pallas_call(functools.partial(last, scale), grid=(4,), out_shape=[jax....]
    unnamed x1 -> x8, local copies, waits for them, and re-layouts: 3.18 us -> 3.68 us
where the time goes in v3:
time: 103 us; the launch traced here: 102 us
  Pallas kernels  98.1 us (95%)
  local copies, waits for them, and re-layouts  3.68 us (4%)
    pallas_call x1, Pallas kernels, shards(): pl.pallas_call(functools.partial(kernel, n_dp), out_shape=[jax.ShapeDtype...  93.5 us
    pallas_call x1, Pallas kernels, shards(): pl.pallas_call(functools.partial(last, scale), grid=(4,), out_shape=[jax....  4.57 us
    unnamed x8, local copies, waits for them, and re-layouts  3.68 us

profile of v3, /device:TPU:1, one launch (start us, length us, event | category | flops | bytes accessed | tf_op | source)
XLA Modules:
  0.0 102.4 jit_solution(6220913373132357154)
XLA Ops:
  0.6 0.0 copy-start.3
  0.6 93.5 %shard_map.93 = (bf16[128,1024]{1,0:T(8,128)(2,1)}, bf16[512,384]{1,0:T(8,128)(2,1)}, bf16[5,1024,256]{2,1,0:T(8,128)(2,1)}) custom-call(bf16[128,1024]{1,0:T(8,128)(2,1)} %tok_h.1, bf16[128,1024]{1,0:T(8,128)(2,1)} %cot_h.1, s32[1,128]{1,0:T(1,128)} %bitcast.1, s32[1,512]{1,0:T(1,128)} %seg_ref.1, bf16[1024,4,256]{2,1,0:T(4,128)(2,1)} %w_h.1, ...), custom_call_target="tpu_custom_call" | custom-call | flops 6000000000 | bytes 12000000 | tf_op jit(solution)/shard_map/pallas_call | solution.py:654
  94.1 0.0 copy-done.3
  94.2 0.0 copy-start
  94.2 1.7 %copy-done = bf16[5,1024,256]{2,1,0:T(8,128)(2,1)S(1)} copy-done((bf16[5,1024,256]{2,1,0:T(8,128)(2,1)S(1)}, bf16[5,1024,256]{2,1,0:T(8,128)(2,1)}, u32[]{:S(2)}) %copy-start) | copy-done | bytes 2621464
  95.9 0.0 copy-start.1
  95.9 1.0 copy-done.1
  96.9 0.0 copy-start.2
  96.9 0.9 copy-done.2
  97.8 4.6 %shard_map.94 = (bf16[128,1024]{1,0:T(8,128)(2,1)}, bf16[128,1024]{1,0:T(8,128)(2,1)}, f32[1024,4,256]{2,1,0:T(4,128)}, f32[256,1024]{1,0:T(8,128)}) custom-call(bf16[128,1024]{1,0:T(8,128)(2,1)S(1)} %copy-done.2, bf16[512,384]{1,0:T(8,128)(2,1)S(1)} %copy-done.1, s32[1,128]{1,0:T(1,128)S(1)} %bitcast.2, bf16[5,1024,256]{2,1,0:T(8,128)(2,1)S(1)} %copy-done), custom_call_target="tpu_custom_call" | custom-call | flops 100000000 | bytes 10000000 | tf_op jit(solution)/shard_map/pallas_call | solution.py:670
Async XLA Ops:
  0.6 93.5 %copy-start.3 = (s32[128]{0:T(128)S(1)}, s32[128]{0:T(128)}, u32[]{:S(2)}) copy-start(s32[128]{0:T(128)} %param.8) | copy-start | bytes 1540
  94.2 1.7 %copy-start = (bf16[5,1024,256]{2,1,0:T(8,128)(2,1)S(1)}, bf16[5,1024,256]{2,1,0:T(8,128)(2,1)}, u32[]{:S(2)}) copy-start(bf16[5,1024,256]{2,1,0:T(8,128)(2,1)} %get-tuple-element.9.ar) | copy-start | bytes 7864324
  95.9 1.0 copy-start.1
  96.9 0.9 copy-start.2

commit v4 on v3

--- a/solution.py
+++ b/solution.py
@@ -248,21 +248,21 @@
 
     def project(block):
         rows = pl.ds(al(block, 128), 128)
-        nT = jnp.transpose(nrm[rows, :].astype(f32)).astype(bf16)
-        nrm_t[block] = nT
-
-        @pl.loop(0, 4)
-        def _(h):
+        for h in range(4):
             pre = dot(nrm[rows, :], w[h])
             sig = sigmoid(pre)
             act = pre * sig
-            slope[h, rows, :] = sig * (1.0 + pre * (1.0 - sig))
+            slope[h, rows, :] = sig + act * (1.0 - sig)
             uv[h, rows, :] = act[:, :128].astype(bf16)
             b = act[:, 128:].astype(bf16)
             qk[h, rows, :] = b
             bf = b.astype(f32)
             kq[h, rows, :] = pltpu.roll(bf, 64, 1).astype(bf16)
-            qz[h, rows, :] = jnp.where(lane_lo, bf * 0.125, 0.0).astype(bf16)
+            qz[h, rows, :] = jnp.where(lane_lo, bf * 0.0625, 0.0).astype(bf16)
+
+    def turn():
+        for b in range(4):
+            nrm_t[:, b * 128:b * 128 + 128] = jnp.transpose(nrm[b * 128:b * 128 + 128, :].astype(f32)).astype(bf16)
 
     n_start, n_forward, n_near, n_far = ag(0, nrm)
     g_start, g_forward, g_near, g_far = ag(1, gbuf)
@@ -292,12 +292,13 @@
             for b in range(4):
                 r, n = slice(b * 128, b * 128 + 128), (b + 1) * 128
                 t = dot_nt(qz[h, r, :], kq[h, :n, :])
-                sig = sigmoid(t)
+                th = jnp.tanh(t)
                 m = msk[r, :n]
-                pw = t * sig
+                up = 1.0 + th
+                pw = t * up
                 p = (pw * m).astype(bf16)
                 p_ref[h, r, :n] = p
-                sl_ref[h, r, :n] = ((sig + pw * (1.0 - sig)) * (m * 0.125)).astype(bf16)
+                sl_ref[h, r, :n] = ((up + pw * (1.0 - th)) * m).astype(bf16)
                 pv = dot(p, uv[h, :n, :]).astype(bf16).astype(f32)
                 u_here = uv[h, r, :].astype(f32)
                 if half_j == 0:
@@ -330,6 +331,7 @@
         rc(st_all.at[cx], st_all.at[cx], st_s, st_r, {"ctx": lax.rem(cx + o, 4)}).start()
     sends.append(lambda: wait_bytes(st_all.at[pl.ds(0, 3)], st_s, st_r).wait_send())
     flight["st"] = lambda: wait_bytes(st_all.at[pl.ds(0, 3)], st_s, st_r).wait_recv()
+    turn()
     arrive("st")
     ms = [st_all[l, 0:1, :] for l in range(4)]
     m2 = (ms[0] + ms[1] + ms[2] + ms[3]) * 0.25
@@ -481,18 +483,14 @@
             dv = dot_tn(p_ref[h, c, r], dout[h, c, :])
             dk = dot_tn(ds_ref[c, r], qk[h, c, :])
             d1 = jnp.where(lane_lo, du_ref[h, r, :], dv)
-            d2 = pltpu.roll(jnp.where(lane_lo, dk, dq_ref[r, :]), 64, 1)
+            d2 = pltpu.roll(jnp.where(lane_lo, dk, dq_ref[r, :]), 64, 1) * 0.0625
             dpre[h, r, 0:128] = (d1 * slope[h, r, 0:128]).astype(bf16)
             dpre[h, r, 128:256] = (d2 * slope[h, r, 128:256]).astype(bf16)
 
     def piece(h):
-        @pl.loop(0, 4)
-        def _(q):
-            acc = jnp.zeros((256, 256), f32)
-            for b in range(4):
-                acc = acc + dot(nrm_t[b, pl.ds(al(q, 256), 256), :], dpre[h, b * 128:b * 128 + 128, :])
-            ar_src[h + 1, pl.ds(al(q, 256), 256), :] = acc.astype(bf16)
-
+        for q in range(4):
+            acc = dot(nrm_t[q * 256:q * 256 + 256, :], dpre[h])
+            ar_src[h + 1, q * 256:q * 256 + 256, :] = acc.astype(bf16)
         ar1(h + 1)
 
     def dnorm(block, dst):
@@ -521,25 +519,14 @@
         ar_src[0, cb * 256:cb * 256 + 256, :] = dot_tn(gated[...], gbuf[:, cb * 256:cb * 256 + 256]).astype(bf16)
     ar1(0)
     backward(1)
+    ar2(1)
     piece(1)
-    ar2(1)
-    arrive("gt")
-    for cb in range(4):
-        s = slice(cb * 256, cb * 256 + 256)
-        acc = xp[:, s].astype(f32)
-        for c in range(4):
-            acc = acc + dot(gfull[c * 128:c * 128 + 128, :], wo[c * 256:c * 256 + 256, s])
-        yd[:, s] = acc.astype(bf16)
-    pack_back(yd, send_y)
-    a2a_start(2, send_y, recv_y)
-
     ar2(0)
+    backward(2)
+    ar2(2)
     ar3(1)
-    backward(2)
     piece(2)
-    ar2(2)
     ar3(0)
-    ar4(1)
     backward(3)
 
     to_far, to_right, to_left = rs_send.at[0], rs_send.at[1], rs_send.at[2]
@@ -553,8 +540,8 @@
     piece(3)
     ar2(3)
     ar3(2)
+    ar4(1)
     ar4(0)
-    ar5(1)
     arrive(("rs", 0))
     to_right[lo, :] = (to_right[lo, :].astype(f32) + rs1[0].astype(f32)).astype(bf16)
     rs_go(to_right.at[lo], rs2.at[0, lo], 4, right)
@@ -564,12 +551,23 @@
     ar2(4)
     ar3(3)
     ar4(2)
+    ar5(1)
     ar5(0)
-    ar6(1)
+    arrive("gt")
+    for cb in range(4):
+        s = slice(cb * 256, cb * 256 + 256)
+        acc = xp[:, s].astype(f32)
+        for c in range(4):
+            acc = acc + dot(gfull[c * 128:c * 128 + 128, :], wo[c * 256:c * 256 + 256, s])
+        yd[:, s] = acc.astype(bf16)
+    pack_back(yd, send_y)
+    a2a_start(2, send_y, recv_y)
+
     dnorm(cx, rs_own)
     ar3(4)
     ar4(3)
     ar5(2)
+    ar6(1)
     ar6(0)
     arrive(("rs", 2), ("rs", 3), ("rs", 4), ("rs", 5))
     dn = rs_own[...] + rs2[0].astype(f32) + rs2[1].astype(f32)
@@ -629,7 +627,7 @@
         vmem((512, 384), bf16),
         vmem((8, 512), f32), vmem((128, 128), i32),
         vmem((128, 1024), bf16), vmem((128, 1024), f32), vmem((128, 128), f32),
-        vmem((512, 1024), bf16), vmem((4, 1024, 128), bf16), vmem((512, 1024), bf16),
+        vmem((512, 1024), bf16), vmem((1024, 512), bf16), vmem((512, 1024), bf16),
         vmem((512, 512), f32), vmem((4, 512, 256), f32),
         vmem((4, 512, 128), bf16), vmem((4, 512, 128), bf16),
         vmem((4, 512, 128), bf16), vmem((4, 512, 128), bf16),
@@ -688,7 +686,7 @@
             pl.BlockSpec((256, 4, 256), lambda i: (i, 0, 0)),
             pl.BlockSpec((256, 256), lambda i: (0, i)),
         ],
-        compiler_params=pltpu.CompilerParams(vmem_limit_bytes=40 * 1024 * 1024),
+        compiler_params=pltpu.CompilerParams(vmem_limit_bytes=60 * 1024 * 1024),
         cost_estimate=pl.CostEstimate(flops=10**8, bytes_accessed=10 * 10**6, transcendentals=0),
     )(y, dx, pos, ar)
 

time: 103 us -> 97.9 us (0.950)
  local copies, waits for them, and re-layouts: 3.68 us -> 0 us
    unnamed x8 -> x0, local copies, waits for them, and re-layouts: 3.68 us -> none
    pallas_call x1, Pallas kernels: 93.5 us -> 90.7 us  [shards(): pl.pallas_call(functools.partial(kernel, n_dp), out_shape=[jax.ShapeDtype...]
    pallas_call x1, Pallas kernels: 4.57 us -> 6.34 us  [shards(): pl.pallas_call(functools.partial(last, scale), grid=(4,), out_shape=[jax....]
where the time goes in v4:
time: 97.9 us; the launch traced here: 97.7 us
  Pallas kernels  97.1 us (99%)
    pallas_call x1, Pallas kernels, shards(): pl.pallas_call(functools.partial(kernel, n_dp), out_shape=[jax.ShapeDtype...  90.7 us
    pallas_call x1, Pallas kernels, shards(): pl.pallas_call(functools.partial(last, scale), grid=(4,), out_shape=[jax....  6.34 us

profile of v4, /device:TPU:1, one launch (start us, length us, event | category | flops | bytes accessed | tf_op | source)
XLA Modules:
  0.0 97.7 jit_solution(14072555706340058391)
XLA Ops:
  0.6 90.7 %shard_map.93 = (bf16[128,1024]{1,0:T(8,128)(2,1)}, bf16[512,384]{1,0:T(8,128)(2,1)}, bf16[5,1024,256]{2,1,0:T(8,128)(2,1)}) custom-call(bf16[128,1024]{1,0:T(8,128)(2,1)} %tok_h.1, bf16[128,1024]{1,0:T(8,128)(2,1)} %cot_h.1, s32[1,128]{1,0:T(1,128)} %bitcast.1, s32[1,512]{1,0:T(1,128)} %seg_ref.1, bf16[1024,4,256]{2,1,0:T(4,128)(2,1)} %w_h.1, ...), custom_call_target="tpu_custom_call" | custom-call | flops 6000000000 | bytes 12000000 | tf_op jit(solution)/shard_map/pallas_call | solution.py:652
  91.4 6.3 %shard_map.94 = (bf16[128,1024]{1,0:T(8,128)(2,1)}, bf16[128,1024]{1,0:T(8,128)(2,1)}, f32[1024,4,256]{2,1,0:T(4,128)}, f32[256,1024]{1,0:T(8,128)}) custom-call(bf16[128,1024]{1,0:T(8,128)(2,1)} %get-tuple-element.7.y, bf16[512,384]{1,0:T(8,128)(2,1)} %get-tuple-element.8.recv, s32[1,128]{1,0:T(1,128)} %bitcast.2, bf16[5,1024,256]{2,1,0:T(8,128)(2,1)} %get-tuple-element.9.ar), custom_call_target="tpu_custom_call" | custom-call | flops 100000000 | bytes 10000000 | tf_op jit(solution)/shard_map/pallas_call | solution.py:668

commit v5 on v4

--- a/solution.py
+++ b/solution.py
@@ -283,7 +283,6 @@
     project(left)
     project(right)
     n_far()
-    g_start()
     project(opp)
 
     for j in range(2):
@@ -310,7 +309,6 @@
                         lane_lo, u_ref[r, j * 128:j * 128 + 128], pltpu.roll(u_here, 64, 1)
                     )
 
-    g_forward()
     arrive("dg")
 
     @pl.loop(0, 4)
@@ -333,6 +331,7 @@
     flight["st"] = lambda: wait_bytes(st_all.at[pl.ds(0, 3)], st_s, st_r).wait_recv()
     turn()
     arrive("st")
+    g_start()
     ms = [st_all[l, 0:1, :] for l in range(4)]
     m2 = (ms[0] + ms[1] + ms[2] + ms[3]) * 0.25
     sq, se, seo = 0.0, 0.0, 0.0
@@ -496,12 +495,12 @@
     def dnorm(block, dst):
         rows = pl.ds(al(block, 128), 128)
 
-        @pl.loop(0, 4)
-        def _(cb):
-            acc = jnp.zeros((128, 256), f32)
-            for h in range(4):
-                acc = acc + dot_nt(dpre[h, rows, :], w[h, pl.ds(al(cb, 256), 256), :])
-            dst[:, pl.ds(al(cb, 256), 256)] = acc.astype(dst.dtype)
+        for cb in range(4):
+            s = slice(cb * 256, cb * 256 + 256)
+            acc = dot_nt(dpre[0, rows, :], w[0, s, :])
+            for h in range(1, 4):
+                acc = acc + dot_nt(dpre[h, rows, :], w[h, s, :])
+            dst[:, s] = acc.astype(dst.dtype)
 
     lo, hi = pl.ds(0, 64), pl.ds(64, 64)
 
@@ -513,20 +512,14 @@
 
     backward(0)
     piece(0)
-    g_near()
-    g_far()
-    for cb in range(4):
-        ar_src[0, cb * 256:cb * 256 + 256, :] = dot_tn(gated[...], gbuf[:, cb * 256:cb * 256 + 256]).astype(bf16)
-    ar1(0)
     backward(1)
     ar2(1)
     piece(1)
-    ar2(0)
+    g_forward()
     backward(2)
     ar2(2)
+    piece(2)
     ar3(1)
-    piece(2)
-    ar3(0)
     backward(3)
 
     to_far, to_right, to_left = rs_send.at[0], rs_send.at[1], rs_send.at[2]
@@ -541,18 +534,21 @@
     ar2(3)
     ar3(2)
     ar4(1)
-    ar4(0)
     arrive(("rs", 0))
     to_right[lo, :] = (to_right[lo, :].astype(f32) + rs1[0].astype(f32)).astype(bf16)
     rs_go(to_right.at[lo], rs2.at[0, lo], 4, right)
     arrive(("rs", 1))
     to_left[hi, :] = (to_left[hi, :].astype(f32) + rs1[1].astype(f32)).astype(bf16)
     rs_go(to_left.at[hi], rs2.at[1, hi], 5, left)
+    g_near()
+    g_far()
+    for cb in range(4):
+        ar_src[0, cb * 256:cb * 256 + 256, :] = dot_tn(gated[...], gbuf[:, cb * 256:cb * 256 + 256]).astype(bf16)
+    ar1(0)
     ar2(4)
     ar3(3)
     ar4(2)
     ar5(1)
-    ar5(0)
     arrive("gt")
     for cb in range(4):
         s = slice(cb * 256, cb * 256 + 256)
@@ -563,12 +559,16 @@
     pack_back(yd, send_y)
     a2a_start(2, send_y, recv_y)
 
-    dnorm(cx, rs_own)
+    ar2(0)
     ar3(4)
     ar4(3)
     ar5(2)
     ar6(1)
-    ar6(0)
+    dnorm(cx, rs_own)
+    ar3(0)
+    ar4(4)
+    ar5(3)
+    ar6(2)
     arrive(("rs", 2), ("rs", 3), ("rs", 4), ("rs", 5))
     dn = rs_own[...] + rs2[0].astype(f32) + rs2[1].astype(f32)
     xh2 = xhat[...]
@@ -578,14 +578,14 @@
     yd[...] = dx.astype(bf16)
     pack_back(yd, send_d)
     a2a_start(3, send_d, recv_d)
-    ar4(4)
-    ar5(3)
-    ar6(2)
+    ar4(0)
+    ar5(4)
+    ar6(3)
     arrive(("a2a", 2))
     unpack_home(recv_y, y_out)
-    ar5(4)
-    ar6(3)
+    ar5(0)
     ar6(4)
+    ar6(0)
     arrive(("a2a", 3))
     for p in range(PIECES):
         arrive(("ar", 5, p))

time: 97.9 us -> 94.7 us (0.967)
  Pallas kernels: 97.1 us -> 93.9 us
    pallas_call x1, Pallas kernels: 90.7 us -> 87.5 us  [shards(): pl.pallas_call(functools.partial(kernel, n_dp), out_shape=[jax.ShapeDtype...]
where the time goes in v5:
time: 94.7 us; the launch traced here: 94.5 us
  Pallas kernels  93.9 us (99%)
    pallas_call x1, Pallas kernels, shards(): pl.pallas_call(functools.partial(kernel, n_dp), out_shape=[jax.ShapeDtype...  87.5 us
    pallas_call x1, Pallas kernels, shards(): pl.pallas_call(functools.partial(last, scale), grid=(4,), out_shape=[jax....  6.33 us

profile of v5, /device:TPU:1, one launch (start us, length us, event | category | flops | bytes accessed | tf_op | source)
XLA Modules:
  0.0 94.5 jit_solution(5183317527929704003)
XLA Ops:
  0.6 87.5 %shard_map.93 = (bf16[128,1024]{1,0:T(8,128)(2,1)}, bf16[512,384]{1,0:T(8,128)(2,1)}, bf16[5,1024,256]{2,1,0:T(8,128)(2,1)}) custom-call(bf16[128,1024]{1,0:T(8,128)(2,1)} %tok_h.1, bf16[128,1024]{1,0:T(8,128)(2,1)} %cot_h.1, s32[1,128]{1,0:T(1,128)} %bitcast.1, s32[1,512]{1,0:T(1,128)} %seg_ref.1, bf16[1024,4,256]{2,1,0:T(4,128)(2,1)} %w_h.1, ...), custom_call_target="tpu_custom_call" | custom-call | flops 6000000000 | bytes 12000000 | tf_op jit(solution)/shard_map/pallas_call | solution.py:652
  88.2 6.3 %shard_map.94 = (bf16[128,1024]{1,0:T(8,128)(2,1)}, bf16[128,1024]{1,0:T(8,128)(2,1)}, f32[1024,4,256]{2,1,0:T(4,128)}, f32[256,1024]{1,0:T(8,128)}) custom-call(bf16[128,1024]{1,0:T(8,128)(2,1)} %get-tuple-element.7.y, bf16[512,384]{1,0:T(8,128)(2,1)} %get-tuple-element.8.recv, s32[1,128]{1,0:T(1,128)} %bitcast.2, bf16[5,1024,256]{2,1,0:T(8,128)(2,1)} %get-tuple-element.9.ar), custom_call_target="tpu_custom_call" | custom-call | flops 100000000 | bytes 10000000 | tf_op jit(solution)/shard_map/pallas_call | solution.py:668

commit v6 on v5

--- a/solution.py
+++ b/solution.py
@@ -46,7 +46,8 @@
 def kernel(
     n_dp,
     tok_h, cot_h, pos_ref, seg_ref, w_h, wo_h,
-    y_out, recv_d, ar_f,
+    y_hbm, recv_d, ar_hbm,
+    y_out, ar_f, out_s,
     tok, cot, w_raw, w, wo, in_s,
     send_x, recv_x, send_g, recv_g, send_y, recv_y, send_d,
     meta_t, rank_s, xp, xhat, rstd_ref, nrm, nrm_t, gbuf,
@@ -283,6 +284,7 @@
     project(left)
     project(right)
     n_far()
+    g_start()
     project(opp)
 
     for j in range(2):
@@ -331,7 +333,7 @@
     flight["st"] = lambda: wait_bytes(st_all.at[pl.ds(0, 3)], st_s, st_r).wait_recv()
     turn()
     arrive("st")
-    g_start()
+    g_forward()
     ms = [st_all[l, 0:1, :] for l in range(4)]
     m2 = (ms[0] + ms[1] + ms[2] + ms[3]) * 0.25
     sq, se, seo = 0.0, 0.0, 0.0
@@ -470,6 +472,13 @@
         ref = ar_f.at[p, rows_at(base, 512)]
         to_core(5, p, ref, ref)
 
+    stores = []
+
+    def ar7(p):
+        arrive(("ar", 5, p))
+        stores.append(pltpu.make_async_copy(ar_f.at[p], ar_hbm.at[p], out_s.at[p]))
+        stores[-1].start()
+
     def backward(h):
         for b in range(4):
             r, n = slice(b * 128, b * 128 + 128), (b + 1) * 128
@@ -515,7 +524,6 @@
     backward(1)
     ar2(1)
     piece(1)
-    g_forward()
     backward(2)
     ar2(2)
     piece(2)
@@ -581,14 +589,21 @@
     ar4(0)
     ar5(4)
     ar6(3)
+    ar7(1)
+    ar7(2)
     arrive(("a2a", 2))
     unpack_home(recv_y, y_out)
+    stores.append(pltpu.make_async_copy(y_out, y_hbm, out_s.at[PIECES]))
+    stores[-1].start()
     ar5(0)
     ar6(4)
+    ar7(3)
     ar6(0)
+    ar7(4)
+    ar7(0)
     arrive(("a2a", 3))
-    for p in range(PIECES):
-        arrive(("ar", 5, p))
+    for c in stores:
+        c.wait()
     finish()
 
 
@@ -619,6 +634,7 @@
     n_dp = lax.axis_size("dp")
     vmem, sem = pltpu.VMEM, pltpu.SemaphoreType.DMA
     scratch = [
+        vmem((128, 1024), bf16), vmem((PIECES, 1024, 256), bf16), sem((PIECES + 1,)),
         vmem((128, 1024), bf16), vmem((128, 1024), bf16), vmem((1024, 4, 256), bf16), vmem((4, 1024, 256), bf16),
         vmem((1024, 1024), bf16), sem((4,)),
         vmem((512, 512), bf16), vmem((512, 512), bf16),
@@ -657,10 +673,10 @@
             jax.ShapeDtypeStruct((PIECES, 1024, 256), bf16),
         ],
         in_specs=[free, free, spec, spec, free, free],
-        out_specs=[spec] * 3,
+        out_specs=[free, spec, free],
         scratch_shapes=scratch,
         compiler_params=pltpu.CompilerParams(
-            collective_id=0, has_side_effects=True, vmem_limit_bytes=60 * 1024 * 1024
+            collective_id=0, has_side_effects=True, vmem_limit_bytes=44 * 1024 * 1024
         ),
         cost_estimate=pl.CostEstimate(flops=6 * 10**9, bytes_accessed=12 * 10**6, transcendentals=3 * 10**6),
     )(tokens, cotangent, pos, segment_ids, w_proj, w_out)
@@ -686,7 +702,7 @@
             pl.BlockSpec((256, 4, 256), lambda i: (i, 0, 0)),
             pl.BlockSpec((256, 256), lambda i: (0, i)),
         ],
-        compiler_params=pltpu.CompilerParams(vmem_limit_bytes=60 * 1024 * 1024),
+        compiler_params=pltpu.CompilerParams(vmem_limit_bytes=16 * 1024 * 1024),
         cost_estimate=pl.CostEstimate(flops=10**8, bytes_accessed=10 * 10**6, transcendentals=0),
     )(y, dx, pos, ar)
 

time: 94.7 us -> 97.9 us (1.034)
  local copies, waits for them, and re-layouts: 0 us -> 6.41 us
  Pallas kernels: 93.9 us -> 90.5 us
    unnamed x0 -> x12, local copies, waits for them, and re-layouts: none -> 6.41 us
    pallas_call x1, Pallas kernels: 6.33 us -> 4.59 us  [shards(): pl.pallas_call(functools.partial(last, scale), grid=(4,), out_shape=[jax....]
    pallas_call x1, Pallas kernels: 87.5 us -> 86 us  [shards(): pl.pallas_call(functools.partial(kernel, n_dp), out_shape=[jax.ShapeDtype...]
where the time goes in v6:
time: 97.9 us; the launch traced here: 97.6 us
  Pallas kernels  90.5 us (92%)
  local copies, waits for them, and re-layouts  6.41 us (7%)
    pallas_call x1, Pallas kernels, shards(): pl.pallas_call(functools.partial(kernel, n_dp), out_shape=[jax.ShapeDtype...  86 us
    unnamed x12, local copies, waits for them, and re-layouts  6.41 us
    pallas_call x1, Pallas kernels, shards(): pl.pallas_call(functools.partial(last, scale), grid=(4,), out_shape=[jax....  4.59 us

profile of v6, /device:TPU:1, one launch (start us, length us, event | category | flops | bytes accessed | tf_op | source)
XLA Modules:
  0.0 97.6 jit_solution(16652742095310225877)
XLA Ops:
  0.6 0.0 copy-start
  0.6 0.6 copy-done
  1.3 0.0 copy-start.1
  1.3 1.6 %copy-done.1 = bf16[1024,4,256]{2,1,0:T(4,128)(2,1)S(1)} copy-done((bf16[1024,4,256]{2,1,0:T(4,128)(2,1)S(1)}, bf16[1024,4,256]{2,1,0:T(4,128)(2,1)}, u32[]{:S(2)}) %copy-start.1) | copy-done | bytes 2097176
  2.9 0.0 copy-start.2
  2.9 1.6 %copy-done.2 = bf16[1024,1024]{1,0:T(8,128)(2,1)S(1)} copy-done((bf16[1024,1024]{1,0:T(8,128)(2,1)S(1)}, bf16[1024,1024]{1,0:T(8,128)(2,1)}, u32[]{:S(2)}) %copy-start.2) | copy-done | bytes 2097176
  4.5 0.0 copy-start.3
  4.5 0.9 copy-done.3
  5.4 0.0 copy-start.4
  5.4 0.9 copy-done.4
  6.4 0.0 copy-start.5
  6.4 0.7 copy-done.5
  7.1 86.0 %shard_map.93 = (bf16[128,1024]{1,0:T(8,128)(2,1)S(1)}, bf16[512,384]{1,0:T(8,128)(2,1)S(1)}, bf16[5,1024,256]{2,1,0:T(8,128)(2,1)S(1)}) custom-call(bf16[128,1024]{1,0:T(8,128)(2,1)S(1)} %copy-done.3, bf16[128,1024]{1,0:T(8,128)(2,1)S(1)} %copy-done.4, s32[1,128]{1,0:T(1,128)S(1)} %bitcast.1, s32[1,512]{1,0:T(1,128)S(1)} %copy-done.5, ...), custom_call_target="tpu_custom_call" | custom-call | flops 6000000000 | bytes 12000000 | tf_op jit(solution)/shard_map/pallas_call | solution.py:668
  93.0 4.6 %shard_map.94 = (bf16[128,1024]{1,0:T(8,128)(2,1)}, bf16[128,1024]{1,0:T(8,128)(2,1)}, f32[1024,4,256]{2,1,0:T(4,128)}, f32[256,1024]{1,0:T(8,128)}) custom-call(bf16[128,1024]{1,0:T(8,128)(2,1)S(1)} %get-tuple-element.7.y, bf16[512,384]{1,0:T(8,128)(2,1)S(1)} %get-tuple-element.8.recv, s32[1,128]{1,0:T(1,128)S(1)} %bitcast.2, ...), custom_call_target="tpu_custom_call" | custom-call | flops 100000000 | bytes 10000000 | tf_op jit(solution)/shard_map/pallas_call | solution.py:684
Async XLA Ops:
  0.6 0.7 copy-start
  1.3 1.6 %copy-start.1 = (bf16[1024,4,256]{2,1,0:T(4,128)(2,1)S(1)}, bf16[1024,4,256]{2,1,0:T(4,128)(2,1)}, u32[]{:S(2)}) copy-start(bf16[1024,4,256]{2,1,0:T(4,128)(2,1)} %w_h.1) | copy-start | bytes 6291460
  2.9 1.6 %copy-start.2 = (bf16[1024,1024]{1,0:T(8,128)(2,1)S(1)}, bf16[1024,1024]{1,0:T(8,128)(2,1)}, u32[]{:S(2)}) copy-start(bf16[1024,1024]{1,0:T(8,128)(2,1)} %wo_h.1) | copy-start | bytes 6291460
  4.5 0.9 copy-start.3
  5.4 0.9 copy-start.4
  6.4 0.7 copy-start.5

commit v7 on v6

--- a/solution.py
+++ b/solution.py
@@ -524,39 +524,47 @@
     backward(1)
     ar2(1)
     piece(1)
+    g_near()
+    g_far()
+    for cb in range(4):
+        ar_src[0, cb * 256:cb * 256 + 256, :] = dot_tn(gated[...], gbuf[:, cb * 256:cb * 256 + 256]).astype(bf16)
+    ar1(0)
+    ar2(2)
     backward(2)
-    ar2(2)
+    ar3(1)
+    ar2(0)
     piece(2)
-    ar3(1)
+    ar3(2)
     backward(3)
+    ar2(3)
+    ar4(1)
+    ar3(0)
+    piece(3)
 
     to_far, to_right, to_left = rs_send.at[0], rs_send.at[1], rs_send.at[2]
     dnorm(opp, to_far)
     rs_go(to_far.at[lo], rs1.at[0], 0, right)
     rs_go(to_far.at[hi], rs1.at[1], 1, left)
+    ar5(1)
+    ar4(2)
     dnorm(right, to_right)
     rs_go(to_right.at[hi], rs2.at[0, hi], 2, right)
+    ar2(4)
+    ar3(3)
     dnorm(left, to_left)
     rs_go(to_left.at[lo], rs2.at[1, lo], 3, left)
-    piece(3)
-    ar2(3)
-    ar3(2)
-    ar4(1)
+    ar4(0)
+    ar5(2)
     arrive(("rs", 0))
     to_right[lo, :] = (to_right[lo, :].astype(f32) + rs1[0].astype(f32)).astype(bf16)
     rs_go(to_right.at[lo], rs2.at[0, lo], 4, right)
     arrive(("rs", 1))
     to_left[hi, :] = (to_left[hi, :].astype(f32) + rs1[1].astype(f32)).astype(bf16)
     rs_go(to_left.at[hi], rs2.at[1, hi], 5, left)
-    g_near()
-    g_far()
-    for cb in range(4):
-        ar_src[0, cb * 256:cb * 256 + 256, :] = dot_tn(gated[...], gbuf[:, cb * 256:cb * 256 + 256]).astype(bf16)
-    ar1(0)
-    ar2(4)
-    ar3(3)
-    ar4(2)
-    ar5(1)
+    ar3(4)
+    ar4(3)
+    ar5(0)
+    ar6(1)
     arrive("gt")
     for cb in range(4):
         s = slice(cb * 256, cb * 256 + 256)
@@ -567,16 +575,13 @@
     pack_back(yd, send_y)
     a2a_start(2, send_y, recv_y)
 
-    ar2(0)
-    ar3(4)
-    ar4(3)
-    ar5(2)
-    ar6(1)
-    dnorm(cx, rs_own)
-    ar3(0)
     ar4(4)
     ar5(3)
     ar6(2)
+    dnorm(cx, rs_own)
+    ar5(4)
+    ar6(0)
+    ar7(1)
     arrive(("rs", 2), ("rs", 3), ("rs", 4), ("rs", 5))
     dn = rs_own[...] + rs2[0].astype(f32) + rs2[1].astype(f32)
     xh2 = xhat[...]
@@ -586,21 +591,16 @@
     yd[...] = dx.astype(bf16)
     pack_back(yd, send_d)
     a2a_start(3, send_d, recv_d)
-    ar4(0)
-    ar5(4)
     ar6(3)
-    ar7(1)
     ar7(2)
     arrive(("a2a", 2))
     unpack_home(recv_y, y_out)
     stores.append(pltpu.make_async_copy(y_out, y_hbm, out_s.at[PIECES]))
     stores[-1].start()
-    ar5(0)
     ar6(4)
+    ar7(0)
     ar7(3)
-    ar6(0)
     ar7(4)
-    ar7(0)
     arrive(("a2a", 3))
     for c in stores:
         c.wait()
@@ -676,7 +676,7 @@
         out_specs=[free, spec, free],
         scratch_shapes=scratch,
         compiler_params=pltpu.CompilerParams(
-            collective_id=0, has_side_effects=True, vmem_limit_bytes=44 * 1024 * 1024
+            collective_id=0, has_side_effects=True, vmem_limit_bytes=60 * 1024 * 1024
         ),
         cost_estimate=pl.CostEstimate(flops=6 * 10**9, bytes_accessed=12 * 10**6, transcendentals=3 * 10**6),
     )(tokens, cotangent, pos, segment_ids, w_proj, w_out)
@@ -702,7 +702,7 @@
             pl.BlockSpec((256, 4, 256), lambda i: (i, 0, 0)),
             pl.BlockSpec((256, 256), lambda i: (0, i)),
         ],
-        compiler_params=pltpu.CompilerParams(vmem_limit_bytes=16 * 1024 * 1024),
+        compiler_params=pltpu.CompilerParams(vmem_limit_bytes=60 * 1024 * 1024),
         cost_estimate=pl.CostEstimate(flops=10**8, bytes_accessed=10 * 10**6, transcendentals=0),
     )(y, dx, pos, ar)
 

time: 97.9 us -> 89.9 us (0.918)
  local copies, waits for them, and re-layouts: 6.41 us -> 0 us
  Pallas kernels: 90.5 us -> 89.1 us
    unnamed x12 -> x0, local copies, waits for them, and re-layouts: 6.41 us -> none
    pallas_call x1, Pallas kernels: 86 us -> 82.7 us  [shards(): pl.pallas_call(functools.partial(kernel, n_dp), out_shape=[jax.ShapeDtype...]
    pallas_call x1, Pallas kernels: 4.59 us -> 6.34 us  [shards(): pl.pallas_call(functools.partial(last, scale), grid=(4,), out_shape=[jax....]
where the time goes in v7:
time: 89.9 us; the launch traced here: 89.7 us
  Pallas kernels  89.1 us (99%)
    pallas_call x1, Pallas kernels, shards(): pl.pallas_call(functools.partial(kernel, n_dp), out_shape=[jax.ShapeDtype...  82.7 us
    pallas_call x1, Pallas kernels, shards(): pl.pallas_call(functools.partial(last, scale), grid=(4,), out_shape=[jax....  6.34 us

profile of v7, /device:TPU:1, one launch (start us, length us, event | category | flops | bytes accessed | tf_op | source)
XLA Modules:
  0.0 89.7 jit_solution(31320685254678180)
XLA Ops:
  0.6 82.7 %shard_map.93 = (bf16[128,1024]{1,0:T(8,128)(2,1)}, bf16[512,384]{1,0:T(8,128)(2,1)}, bf16[5,1024,256]{2,1,0:T(8,128)(2,1)}) custom-call(bf16[128,1024]{1,0:T(8,128)(2,1)} %tok_h.1, bf16[128,1024]{1,0:T(8,128)(2,1)} %cot_h.1, s32[1,128]{1,0:T(1,128)} %bitcast.1, s32[1,512]{1,0:T(1,128)} %seg_ref.1, bf16[1024,4,256]{2,1,0:T(4,128)(2,1)} %w_h.1, ...), custom_call_target="tpu_custom_call" | custom-call | flops 6000000000 | bytes 12000000 | tf_op jit(solution)/shard_map/pallas_call | solution.py:668
  83.4 6.3 %shard_map.94 = (bf16[128,1024]{1,0:T(8,128)(2,1)}, bf16[128,1024]{1,0:T(8,128)(2,1)}, f32[1024,4,256]{2,1,0:T(4,128)}, f32[256,1024]{1,0:T(8,128)}) custom-call(bf16[128,1024]{1,0:T(8,128)(2,1)} %get-tuple-element.7.y, bf16[512,384]{1,0:T(8,128)(2,1)} %get-tuple-element.8.recv, s32[1,128]{1,0:T(1,128)} %bitcast.2, bf16[5,1024,256]{2,1,0:T(8,128)(2,1)} %get-tuple-element.9.ar), custom_call_target="tpu_custom_call" | custom-call | flops 100000000 | bytes 10000000 | tf_op jit(solution)/shard_map/pallas_call | solution.py:684

commit v8 on v7

--- a/solution.py
+++ b/solution.py
@@ -182,7 +182,6 @@
     a2a_start(0, send_x, recv_x)
     loads[1].wait()
     pack_out(cot, send_g, False)
-    a2a_start(1, send_g, recv_g)
 
     seg_row = seg_ref[...]
     seg_col = jnp.transpose(jnp.broadcast_to(seg_row.astype(f32), (128, GROUP))).astype(i32)
@@ -268,9 +267,14 @@
     n_start, n_forward, n_near, n_far = ag(0, nrm)
     g_start, g_forward, g_near, g_far = ag(1, gbuf)
     n_start()
+    a2a_start(1, send_g, recv_g)
+    project(cx)
+    n_forward()
+    n_near()
+    project(left)
+    project(right)
     arrive(("a2a", 1))
     unpack_arrived(recv_g, gbuf, own)
-    n_forward()
     for t in range(4):
         dg_send[t] = dot_nt(gbuf[own, :], wo[t * 256:t * 256 + 256, :]).astype(bf16)
     for o in (2, 1, 3):
@@ -279,10 +283,6 @@
     sends.append(lambda: wait_bytes(dg_ref.at[pl.ds(0, 384)], dg_s, dg_r).wait_send())
     flight["dg"] = lambda: wait_bytes(dg_ref.at[pl.ds(0, 384)], dg_s, dg_r).wait_recv()
     dg_ref[own, :] = dg_send[cx]
-    project(cx)
-    n_near()
-    project(left)
-    project(right)
     n_far()
     g_start()
     project(opp)

time: 89.9 us -> 88.4 us (0.983)
  Pallas kernels: 89.1 us -> 87.5 us
    pallas_call x1, Pallas kernels: 82.7 us -> 81.2 us  [shards(): pl.pallas_call(functools.partial(kernel, n_dp), out_shape=[jax.ShapeDtype...]
where the time goes in v8:
time: 88.4 us; the launch traced here: 88.2 us
  Pallas kernels  87.5 us (99%)
    pallas_call x1, Pallas kernels, shards(): pl.pallas_call(functools.partial(kernel, n_dp), out_shape=[jax.ShapeDtype...  81.2 us
    pallas_call x1, Pallas kernels, shards(): pl.pallas_call(functools.partial(last, scale), grid=(4,), out_shape=[jax....  6.33 us

profile of v8, /device:TPU:1, one launch (start us, length us, event | category | flops | bytes accessed | tf_op | source)
XLA Modules:
  0.0 88.2 jit_solution(11176620119762314861)
XLA Ops:
  0.6 81.2 %shard_map.93 = (bf16[128,1024]{1,0:T(8,128)(2,1)}, bf16[512,384]{1,0:T(8,128)(2,1)}, bf16[5,1024,256]{2,1,0:T(8,128)(2,1)}) custom-call(bf16[128,1024]{1,0:T(8,128)(2,1)} %tok_h.1, bf16[128,1024]{1,0:T(8,128)(2,1)} %cot_h.1, s32[1,128]{1,0:T(1,128)} %bitcast.1, s32[1,512]{1,0:T(1,128)} %seg_ref.1, bf16[1024,4,256]{2,1,0:T(4,128)(2,1)} %w_h.1, ...), custom_call_target="tpu_custom_call" | custom-call | flops 6000000000 | bytes 12000000 | tf_op jit(solution)/shard_map/pallas_call | solution.py:668
  81.8 6.3 %shard_map.94 = (bf16[128,1024]{1,0:T(8,128)(2,1)}, bf16[128,1024]{1,0:T(8,128)(2,1)}, f32[1024,4,256]{2,1,0:T(4,128)}, f32[256,1024]{1,0:T(8,128)}) custom-call(bf16[128,1024]{1,0:T(8,128)(2,1)} %get-tuple-element.7.y, bf16[512,384]{1,0:T(8,128)(2,1)} %get-tuple-element.8.recv, s32[1,128]{1,0:T(1,128)} %bitcast.2, bf16[5,1024,256]{2,1,0:T(8,128)(2,1)} %get-tuple-element.9.ar), custom_call_target="tpu_custom_call" | custom-call | flops 100000000 | bytes 10000000 | tf_op jit(solution)/shard_map/pallas_call | solution.py:684

commit v9 on v8

--- a/solution.py
+++ b/solution.py
@@ -573,13 +573,13 @@
             acc = acc + dot(gfull[c * 128:c * 128 + 128, :], wo[c * 256:c * 256 + 256, s])
         yd[:, s] = acc.astype(bf16)
     pack_back(yd, send_y)
-    a2a_start(2, send_y, recv_y)
 
     ar4(4)
     ar5(3)
     ar6(2)
     dnorm(cx, rs_own)
     ar5(4)
+    a2a_start(2, send_y, recv_y)
     ar6(0)
     ar7(1)
     arrive(("rs", 2), ("rs", 3), ("rs", 4), ("rs", 5))

time: 88.4 us -> 90.6 us (1.025)
  Pallas kernels: 87.5 us -> 89.8 us
    pallas_call x1, Pallas kernels: 81.2 us -> 83.4 us  [shards(): pl.pallas_call(functools.partial(kernel, n_dp), out_shape=[jax.ShapeDtype...]
where the time goes in v9:
time: 90.6 us; the launch traced here: 90.4 us
  Pallas kernels  89.8 us (99%)
    pallas_call x1, Pallas kernels, shards(): pl.pallas_call(functools.partial(kernel, n_dp), out_shape=[jax.ShapeDtype...  83.4 us
    pallas_call x1, Pallas kernels, shards(): pl.pallas_call(functools.partial(last, scale), grid=(4,), out_shape=[jax....  6.33 us

profile of v9, /device:TPU:1, one launch (start us, length us, event | category | flops | bytes accessed | tf_op | source)
XLA Modules:
  0.0 90.4 jit_solution(5754103306909571792)
XLA Ops:
  0.6 83.4 %shard_map.93 = (bf16[128,1024]{1,0:T(8,128)(2,1)}, bf16[512,384]{1,0:T(8,128)(2,1)}, bf16[5,1024,256]{2,1,0:T(8,128)(2,1)}) custom-call(bf16[128,1024]{1,0:T(8,128)(2,1)} %tok_h.1, bf16[128,1024]{1,0:T(8,128)(2,1)} %cot_h.1, s32[1,128]{1,0:T(1,128)} %bitcast.1, s32[1,512]{1,0:T(1,128)} %seg_ref.1, bf16[1024,4,256]{2,1,0:T(4,128)(2,1)} %w_h.1, ...), custom_call_target="tpu_custom_call" | custom-call | flops 6000000000 | bytes 12000000 | tf_op jit(solution)/shard_map/pallas_call | solution.py:668
  84.1 6.3 %shard_map.94 = (bf16[128,1024]{1,0:T(8,128)(2,1)}, bf16[128,1024]{1,0:T(8,128)(2,1)}, f32[1024,4,256]{2,1,0:T(4,128)}, f32[256,1024]{1,0:T(8,128)}) custom-call(bf16[128,1024]{1,0:T(8,128)(2,1)} %get-tuple-element.7.y, bf16[512,384]{1,0:T(8,128)(2,1)} %get-tuple-element.8.recv, s32[1,128]{1,0:T(1,128)} %bitcast.2, bf16[5,1024,256]{2,1,0:T(8,128)(2,1)} %get-tuple-element.9.ar), custom_call_target="tpu_custom_call" | custom-call | flops 100000000 | bytes 10000000 | tf_op jit(solution)/shard_map/pallas_call | solution.py:684
